TPU v7x, 32 devices: a whole 2x2x4 slice. The times are simulated.
32 devices in a mesh: groups: 2 (over y), row: 4 (over z), col: 4 (over x, core).
Axes of the slice: x: 2, y: 2, z: 4, core: 2. Of those that a mesh axis runs over, the one named last changes fastest.
Arguments:
- act_train: bfloat16 [1024, 8192], P('groups', 'row'), parts along dimension 0, may hold values from -6 to 6
- act_query: bfloat16 [256, 8192], P('groups', 'row'), parts along dimension 0, may hold values from -6 to 6
- grad_train: bfloat16 [1024, 28672], P('groups', 'col'), parts along dimension 0, may hold values from -6 to 6
- grad_query: bfloat16 [256, 28672], P('groups', 'col'), parts along dimension 0, may hold values from -6 to 6
- basis_in: bfloat16 [16384, 8192], P(('groups', 'row'), 'col'), parts along dimension 0, may hold values from -0.0625 to 0.0625
- basis_out: bfloat16 [57344, 4096], P(('groups', 'col'), 'row'), parts along dimension 0, may hold values from -0.03125 to 0.03125
- correction: float32 [8192, 8192], P(('groups', 'row'), 'col'), parts along dimension 0, may hold values from 0.1 to 2
Outputs:
- scores: float32 [16, 512], P('groups', 'row'), parts along dimension 0
There are 2 independent parts, one for each index of `groups`. A program takes and returns all parts, laid end to end along the dimension named above; each array names one. Nothing has to cross between parts.
All inputs are finite; a program needn't handle non-finite values.
Results may differ from a plain program's by a relative error of at most 0.0054.
Values may be sent and summed in bfloat16 or wider, within the bound.
No kernel may reach another device: no remote copies, remote signals or barrier semaphores. Data moves between devices by JAX's collectives and lax.ppermute only.
A program may use at most 192 MiB of HBM per device.

v0:
```python
import functools

import jax
import jax.numpy as jnp
from jax import lax
from jax.experimental import pallas as pl
from jax.experimental.pallas import tpu as pltpu
from jax.sharding import PartitionSpec as P

I = 8192
O = 4096
NQ = 8
LQ = 16
LANES = 128
CHUNKS = 8
LAG = 3
F32 = jnp.float32
BF16 = jnp.bfloat16
MIB = 1 << 20

VMEM_SPEC = pl.BlockSpec(memory_space=pltpu.VMEM)
SMEM_SPEC = pl.BlockSpec(memory_space=pltpu.SMEM)
ANY_SPEC = pl.BlockSpec(memory_space=pl.ANY)


def shape_of(rows, width, dtype):
    return jax.ShapeDtypeStruct((rows, width), dtype)


def chunk_list(size):
    tiles = size // LANES
    count = min(CHUNKS, tiles)
    chunks, first = [], 0
    for k in range(count):
        width = LANES * (tiles // count + (1 if k < tiles % count else 0))
        chunks.append((first, width))
        first += width
    return chunks


def largest_divisor(size, choices):
    for choice in choices:
        if size % choice == 0:
            return choice
    return size


def pieces_of(width, most):
    return max(p for p in range(1, most + 1) if width % (p * LANES) == 0)


def cost(flops, bytes_accessed):
    return pl.CostEstimate(flops=flops, bytes_accessed=bytes_accessed, transcendentals=0)


def in_hbm(x):
    return pltpu.with_memory_space_constraint(x, pltpu.HBM)


def halves_dot(rows, basis):
    half = rows.shape[0] // 2
    return [jnp.dot(part, basis, preferred_element_type=F32) for part in (rows[:half], rows[half:])]


def in_kernel(chunks, narrow, groups, train_ref, query_ref, basis_ref, prev_ref, *refs):
    count = len(chunks)
    rows_ref, slot_ref, sum_ref, sems = refs[count + narrow :]
    tokens, queries = train_ref.shape[0], query_ref.shape[0]
    start, total = chunks[0][0], slot_ref.shape[2]
    depth = slot_ref.shape[1]
    half = rows_ref.shape[1] // 2

    def copies(g):
        part = pl.ds(pl.multiple_of(g * depth, depth), depth)
        return [
            pltpu.make_async_copy(
                basis_ref.at[part, pl.ds(start, total)], slot_ref.at[g], sems.at[g, 0]
            ),
            pltpu.make_async_copy(
                train_ref.at[:, part], rows_ref.at[g, pl.ds(0, tokens), :], sems.at[g, 1]
            ),
            pltpu.make_async_copy(
                query_ref.at[:, part], rows_ref.at[g, pl.ds(tokens, queries), :], sems.at[g, 2]
            ),
        ]

    for g in range(groups):
        for copy in copies(g):
            copy.start()
    sum_ref[...] = jnp.zeros_like(sum_ref)

    def body(g, carry):
        for copy in copies(g):
            copy.wait()
        for h, value in enumerate(halves_dot(rows_ref[g], slot_ref[g])):
            sum_ref[h * half : (h + 1) * half, :] += value
        return carry

    lax.fori_loop(0, groups, body, 0)
    for j, (first, width) in enumerate(chunks):
        refs[j][...] = sum_ref[:, first - start : first - start + width]
    column = 0
    for narrow_ref in refs[count : count + narrow]:
        width = narrow_ref.shape[1]
        narrow_ref[...] = sum_ref[:, column : column + width].astype(BF16)
        column += width


def in_part(act_train, act_query, basis_in, prev, chunks, narrow):
    tokens, depth = act_train.shape
    rows = tokens + act_query.shape[0]
    total = sum(width for _, width in chunks)
    groups = next(g for g in (4, 2, 1) if depth % (g * LANES) == 0)
    shapes = [shape_of(rows, width, F32) for _, width in chunks]
    shapes += [shape_of(rows, width, BF16) for width in narrow]
    out = pl.pallas_call(
        functools.partial(in_kernel, chunks, len(narrow), groups),
        in_specs=[ANY_SPEC] * 4,
        out_specs=[VMEM_SPEC] * len(shapes),
        out_shape=shapes,
        scratch_shapes=[
            pltpu.VMEM((groups, rows, depth // groups), BF16),
            pltpu.VMEM((groups, depth // groups, total), BF16),
            pltpu.VMEM((rows, total), F32),
            pltpu.SemaphoreType.DMA((groups, 3)),
        ],
        compiler_params=pltpu.CompilerParams(vmem_limit_bytes=24 * MIB),
        cost_estimate=cost(1024, 1024),
    )(in_hbm(act_train), in_hbm(act_query), in_hbm(basis_in), prev)
    return list(out[: len(chunks)]), list(out[len(chunks) :])


def out_kernel(begin, steps, last, train_ref, query_ref, basis_ref, prev_ref, *refs):
    if last:
        start_ref, keep_ref, *give_refs, rows_ref, slot_ref, acc_ref, sems = refs
    else:
        acc_ref, rows_ref, slot_ref, sems = refs
    tokens, queries = train_ref.shape[0], query_ref.shape[0]
    slots, block = slot_ref.shape[0], slot_ref.shape[1]
    half, width = acc_ref.shape[0] // 2, acc_ref.shape[1]
    tile = largest_divisor(width, (256, 128))

    def copies(step):
        slot = lax.rem(step, slots)
        part = pl.ds(pl.multiple_of((begin + step) * block, block), block)
        return [
            pltpu.make_async_copy(basis_ref.at[part, :], slot_ref.at[slot], sems.at[slot, 0]),
            pltpu.make_async_copy(
                train_ref.at[:, part], rows_ref.at[slot, pl.ds(0, tokens), :], sems.at[slot, 1]
            ),
            pltpu.make_async_copy(
                query_ref.at[:, part], rows_ref.at[slot, pl.ds(tokens, queries), :], sems.at[slot, 2]
            ),
        ]

    for step in range(min(slots - 1, steps)):
        for copy in copies(step):
            copy.start()
    acc_ref[...] = start_ref[...] if last else jnp.zeros_like(acc_ref)

    def body(step, carry):
        for copy in copies(step):
            copy.wait()

        @pl.when(step + slots - 1 < steps)
        def _():
            for copy in copies(step + slots - 1):
                copy.start()

        slot = lax.rem(step, slots)
        rows = rows_ref[slot]
        for first in range(0, width, tile):
            span = slice(first, first + tile)
            acc_ref[:, span] += jnp.dot(rows, slot_ref[slot, :, span], preferred_element_type=F32)
        return carry

    lax.fori_loop(0, steps, body, 0)
    if not last:
        return
    odd = lax.rem(lax.axis_index("col"), 2)
    keep_ref[...] = acc_ref[pl.ds(pl.multiple_of(odd * half, 16), half), :]
    cols = give_refs[0].shape[1]
    for c, give_ref in enumerate(give_refs):
        span = slice(c * cols, (c + 1) * cols)
        give_ref[...] = acc_ref[pl.ds(pl.multiple_of((1 - odd) * half, 16), half), span]


def out_part(grad_train, grad_query, basis_out, prev, acc):
    tokens, depth = grad_train.shape
    width = basis_out.shape[1]
    rows = tokens + grad_query.shape[0]
    block = largest_divisor(depth, (512, 256, 128))
    steps = depth // block
    slots = min(6, steps)
    last = acc is not None
    first = steps * 2 // 7
    begin, count = (first, steps - first) if last else (0, first)
    pieces = pieces_of(width, 2)
    if last:
        out_shape = [shape_of(rows // 2, width, F32)]
        out_shape += [shape_of(rows // 2, width // pieces, F32)] * pieces
    else:
        out_shape = [shape_of(rows, width, F32)]
    return pl.pallas_call(
        functools.partial(out_kernel, begin, count, last),
        in_specs=[ANY_SPEC] * 4 + [VMEM_SPEC] * last,
        out_specs=[VMEM_SPEC] * len(out_shape),
        out_shape=out_shape,
        scratch_shapes=[
            pltpu.VMEM((slots, rows, block), BF16),
            pltpu.VMEM((slots, block, width), BF16),
        ]
        + [pltpu.VMEM((rows, width), F32)] * last
        + [pltpu.SemaphoreType.DMA((slots, 3))],
        compiler_params=pltpu.CompilerParams(vmem_limit_bytes=22 * MIB),
        cost_estimate=cost(2 * rows * block * count * width if last else 1024, 1024),
    )(
        in_hbm(grad_train), in_hbm(grad_query), in_hbm(basis_out), prev, *([acc] if last else [])
    )


def by_rows(rows, step):
    block = rows // 5 if rows % 80 == 0 else rows

    def body(i, carry):
        step(pl.ds(pl.multiple_of(i * block, block), block))
        return carry

    lax.fori_loop(0, rows // block, body, 0)


def add_kernel(pieces, outs, cast, keep_ref, *refs):
    wide_ref, narrow_refs = refs[pieces + cast + 1], refs[pieces + cast + 2 :]
    width = keep_ref.shape[1]

    def step(rows):
        total = keep_ref[rows, :]
        got = [refs[c][rows, :].astype(F32) for c in range(pieces)]
        total = total + (jnp.concatenate(got, axis=1) if pieces > 1 else got[0])
        wide_ref[rows, :] = total
        cols = width // outs
        for c in range(outs):
            narrow_refs[c][rows, :] = total[:, c * cols : (c + 1) * cols].astype(BF16)
        if cast:
            narrow_refs[outs][rows, :] = refs[pieces][rows, :].astype(BF16)

    by_rows(keep_ref.shape[0], step)


def add_part(keep, got, prev, outs=1, cast=()):
    rows, width = keep.shape
    out = pl.pallas_call(
        functools.partial(add_kernel, len(got), outs, len(cast)),
        in_specs=[VMEM_SPEC] * (1 + len(got) + len(cast)) + [ANY_SPEC],
        out_specs=[VMEM_SPEC] * (1 + outs + len(cast)),
        out_shape=[shape_of(rows, width, F32)]
        + [shape_of(rows, width // outs, BF16)] * outs
        + [shape_of(*x.shape, BF16) for x in cast],
        compiler_params=pltpu.CompilerParams(vmem_limit_bytes=12 * MIB),
        cost_estimate=cost(1024, 1024),
    )(keep, *got, *cast, prev)
    return out[0], list(out[1:])


def join_kernel(tokens, pieces, prev_ref, *refs):
    mine_refs, other_refs = refs[:pieces], refs[pieces : 2 * pieces]
    gt_ref, gq_ref = refs[2 * pieces :]
    odd = lax.rem(lax.axis_index("col"), 2)
    for c, (mine_ref, other_ref) in enumerate(zip(mine_refs, other_refs)):
        mine, other = mine_ref[...].astype(F32), other_ref[...].astype(F32)
        low = jnp.where(odd == 1, other, mine)
        high = jnp.where(odd == 1, mine, other)
        rows = jnp.concatenate([low, high], axis=0)
        cols = rows.shape[1]
        gt_ref[:, c * cols : (c + 1) * cols] = rows[:tokens].astype(BF16)
        gq_ref[c * cols : (c + 1) * cols, :] = rows[tokens:].T.astype(BF16)


def join_part(mine, other, prev, tokens):
    half = mine[0].shape[0]
    width = sum(x.shape[1] for x in mine)
    queries = 2 * half - tokens
    return pl.pallas_call(
        functools.partial(join_kernel, tokens, len(mine)),
        in_specs=[ANY_SPEC] + [VMEM_SPEC] * (2 * len(mine)),
        out_specs=[VMEM_SPEC] * 2,
        out_shape=[shape_of(tokens, width, BF16), shape_of(width, queries, BF16)],
        compiler_params=pltpu.CompilerParams(vmem_limit_bytes=12 * MIB),
        cost_estimate=cost(1024, 1024),
    )(prev, *mine, *other)


def inverse_kernel(chunks, corr_ref, prev_ref, *refs):
    *inv_refs, slot_ref, sems = refs
    slots, block = slot_ref.shape[0], slot_ref.shape[1]
    steps = corr_ref.shape[0] // block

    def fetch(step):
        slot = lax.rem(step, slots)
        rows = pl.ds(pl.multiple_of(step * block, block), block)
        return pltpu.make_async_copy(corr_ref.at[rows, :], slot_ref.at[slot], sems.at[slot])

    for step in range(min(slots, steps)):
        fetch(step).start()

    def body(step, carry):
        fetch(step).wait()
        rows = pl.ds(pl.multiple_of(step * block, block), block)
        slot = lax.rem(step, slots)
        for (first, width), inv_ref in zip(chunks, inv_refs):
            inv_ref[rows, :] = 1.0 / slot_ref[slot, :, first : first + width]

        @pl.when(step + slots < steps)
        def _():
            fetch(step + slots).start()

        return carry

    lax.fori_loop(0, steps, body, 0)


def inverse_part(correction, prev, chunks):
    rows, width = correction.shape
    block = largest_divisor(rows, (128, 64, 8))
    out = pl.pallas_call(
        functools.partial(inverse_kernel, chunks),
        in_specs=[ANY_SPEC, ANY_SPEC],
        out_specs=[VMEM_SPEC] * len(chunks),
        out_shape=[shape_of(rows, width, F32) for _, width in chunks],
        scratch_shapes=[pltpu.VMEM((4, block, width), F32), pltpu.SemaphoreType.DMA((4,))],
        compiler_params=pltpu.CompilerParams(vmem_limit_bytes=16 * MIB),
        cost_estimate=cost(1024, 1024),
    )(in_hbm(correction), prev)
    return list(out)


def at_end():
    me = lax.axis_index("row")
    return (me == 0) | (me == lax.axis_size("row") - 1)


def pay_kernel(has_part, acc_ref, got_ref, *refs):
    end = at_end()

    def step(rows):
        total = acc_ref[rows, :] + got_ref[rows, :].astype(F32)
        if has_part:
            total = jnp.where(end, refs[0][rows, :], total)
        refs[-1][rows, :] = total.astype(BF16)

    by_rows(acc_ref.shape[0], step)


def pay_part(hint, acc, got, part, prev):
    has_part = part is not None
    return pl.pallas_call(
        functools.partial(pay_kernel, has_part),
        in_specs=[VMEM_SPEC, VMEM_SPEC] + [VMEM_SPEC] * has_part + [ANY_SPEC],
        out_specs=VMEM_SPEC,
        out_shape=shape_of(*acc.shape, BF16),
        compiler_params=pltpu.CompilerParams(vmem_limit_bytes=12 * MIB),
        cost_estimate=cost(hint, 1024),
    )(acc, got, *([part] if has_part else []), prev)


def after_kernel(first_ref, second_ref, out_ref):
    out_ref[...] = jnp.zeros_like(out_ref)


def after_part(first, second):
    return pl.pallas_call(
        after_kernel,
        in_specs=[ANY_SPEC] * 2,
        out_specs=VMEM_SPEC,
        out_shape=shape_of(8, LANES, F32),
        compiler_params=pltpu.CompilerParams(vmem_limit_bytes=4 * MIB),
        cost_estimate=cost(10**9, 1024),
    )(first, second)


def score_kernel(
    start, scale, outs, gt_ref, gq_ref, inv_ref, sent_ref, got_ref, prev_ref, order_ref, *refs
):
    out_refs = refs[:outs]
    quot_ref, wide_ref, own_ref = refs[outs:]
    tokens = gt_ref.shape[0]
    queries = gq_ref.shape[1]
    width = inv_ref.shape[1]
    total = jnp.where(at_end(), got_ref[...].astype(F32), sent_ref[...].astype(F32))
    wide_ref[...] = total[:tokens]
    own_ref[...] = total[tokens:]
    owner = lax.broadcasted_iota(jnp.int32, (queries, width), 0) // LQ
    lane = lax.broadcasted_iota(jnp.int32, (tokens, LANES), 1)

    def quotient(q):
        own = jnp.where(owner == q, own_ref[...], 0.0).astype(BF16)
        products = jnp.dot(gq_ref[...], own, preferred_element_type=F32)
        quot_ref[q % 2] = (products * inv_ref[...]).astype(BF16)

    quotient(0)
    result = jnp.zeros((tokens, LANES), F32) if start else prev_ref[...]
    for q in range(NQ):
        if q + 1 < NQ:
            quotient(q + 1)
        mapped = jnp.dot(gt_ref[...], quot_ref[q % 2], preferred_element_type=F32)
        scaled = mapped * wide_ref[...]
        folded = scaled[:, :LANES]
        for part in range(1, width // LANES):
            folded = folded + scaled[:, part * LANES : (part + 1) * LANES]
        result = result + jnp.where(lane == q, jnp.sum(folded, axis=1, keepdims=True), 0.0)
    if scale is None:
        out_refs[0][...] = result
        return
    final = (result * scale).T[:NQ]
    if outs == 1:
        out_refs[0][...] = final
        return
    me = lax.axis_index("row")
    cols = final.shape[1] // outs
    for step, out_ref in enumerate(out_refs):
        block = final[:, :cols]
        for other in range(1, outs):
            own = final[:, other * cols : (other + 1) * cols]
            block = jnp.where(jnp.bitwise_xor(me, step) == other, own, block)
        out_ref[...] = block


def score_part(rot_gt, rot_gq_t, inv, sent, got, prev, order, start, scale, halves):
    tokens, outs = rot_gt.shape
    width = inv.shape[1]
    queries = rot_gq_t.shape[1]
    if scale is None:
        out_shape = [shape_of(tokens, LANES, F32)]
    elif halves:
        out_shape = [shape_of(NQ, tokens // halves, F32)] * halves
    else:
        out_shape = [shape_of(NQ, tokens, F32)]
    return pl.pallas_call(
        functools.partial(score_kernel, start, scale, len(out_shape)),
        in_specs=[VMEM_SPEC] * 5 + [ANY_SPEC if start else VMEM_SPEC, ANY_SPEC],
        out_specs=[VMEM_SPEC] * len(out_shape),
        out_shape=out_shape,
        scratch_shapes=[
            pltpu.VMEM((2, outs, width), BF16),
            pltpu.VMEM((tokens, width), F32),
            pltpu.VMEM((queries, width), F32),
        ],
        compiler_params=pltpu.CompilerParams(vmem_limit_bytes=16 * MIB),
        cost_estimate=cost(1024, 1024),
    )(rot_gt, rot_gq_t, inv, sent, got, prev, order)


def gather_kernel(*refs):
    total = refs[0][...]
    for ref in refs[1:-1]:
        total = total + ref[...]
    refs[-1][...] = total


def gather_part(arrays):
    return pl.pallas_call(
        gather_kernel,
        in_specs=[VMEM_SPEC] * len(arrays),
        out_specs=VMEM_SPEC,
        out_shape=shape_of(*arrays[0].shape, F32),
        compiler_params=pltpu.CompilerParams(vmem_limit_bytes=4 * MIB),
        cost_estimate=cost(1024, 1024),
    )(*arrays)


def line_sum(partial, axis):
    n = lax.axis_size(axis)
    half = n // 2
    me = lax.axis_index(axis)
    if n % 2:
        return lax.psum(partial, axis).astype(BF16)
    acc = partial
    for s in range(half - 1):
        pairs = [(s, s + 1), (n - 1 - s, n - 2 - s)]
        acc = acc + lax.ppermute(acc.astype(BF16), axis, pairs).astype(F32)
    got = lax.ppermute(acc.astype(BF16), axis, [(half - 1, half), (half, half - 1)])
    total = (acc + got.astype(F32)).astype(BF16)
    for s in range(half - 2, -1, -1):
        pairs = [(s + 1, s), (n - 2 - s, n - 1 - s)]
        got = lax.ppermute(total, axis, pairs)
        total = jnp.where((me == s) | (me == n - 1 - s), got, total)
    return total


def owned_sum(partial, axis):
    n = lax.axis_size(axis)
    me = lax.axis_index(axis)
    total = lax.dynamic_index_in_dim(partial, me, 0, keepdims=False)
    for step in range(1, n):
        block = lax.dynamic_index_in_dim(partial, (me + step) % n, 0, keepdims=False)
        total = total + lax.ppermute(block, axis, [(d, (d + step) % n) for d in range(n)])
    return total


def shared_sum(partial, axis):
    n = lax.axis_size(axis)
    total = partial
    for step in range(1, n):
        total = total + lax.ppermute(partial, axis, [(d, (d + step) % n) for d in range(n)])
    return total


def on_device(act_train, act_query, grad_train, grad_query, basis_in, basis_out, correction):
    norm_scale = (O * I * LQ) ** (-0.5)
    tokens = act_train.shape[0]
    n_row, n_col = lax.axis_size("row"), lax.axis_size("col")
    chunks = chunk_list(basis_in.shape[1])
    count = len(chunks)
    line = n_row == 4
    flip = [(d, d ^ 1) for d in range(n_col)]
    outer = [(0, 1), (1, 0), (2, 3), (3, 2)]
    inner = []
    for c in range(n_col):
        inner += [(n_col + c, 2 * n_col + c), (2 * n_col + c, n_col + c)]
        inner += [(c, c ^ 1), (3 * n_col + c, 3 * n_col + (c ^ 1))]
    sent, got, acc, got_mid = {}, {}, {}, {}

    def swap(j, payload):
        sent[j] = payload
        got[j] = lax.ppermute(payload, "row", outer)

    def meet(j, prev):
        if not line or j >= count:
            return prev
        cast = [parts[2]] if j == 0 else []
        acc[j], thin = add_part(parts[j], [got[j]], prev, 1, cast)
        got_mid[j] = lax.ppermute(thin[0], ("row", "col"), inner)
        if cast:
            swap(2, thin[1])
        return thin[0]

    def pay(j, prev):
        if not line:
            sent[j + LAG] = got[j + LAG] = line_sum(parts[j], "row")
            return prev
        part = parts[j + LAG] if j + LAG < count else None
        payload = pay_part(4 * 10**9 if j == 0 else 1024, acc[j], got_mid[j], part, prev)
        swap(j + LAG, payload)
        return payload

    def score(k, sums, prev):
        return score_part(
            rot_gt, rot_gq_t, invs[k], sent[k + LAG], got[k + LAG], sums[0], prev,
            k == 0, norm_scale if k == count - 1 else None, halves,
        )

    early = min(LAG + 2, count)
    widths = [width for _, width in chunks]
    parts, narrow = in_part(
        act_train, act_query, basis_in, act_query, chunks[:1], [widths[0]]
    )
    if line:
        swap(0, narrow[0])
    more, narrow = in_part(
        act_train, act_query, basis_in, parts[0], chunks[1:early], [widths[1]]
    )
    parts += more
    if line:
        swap(1, narrow[0])
    (half_sum,) = out_part(grad_train, grad_query, basis_out, parts[-1], None)
    prev = meet(0, half_sum)
    keep, *give = out_part(grad_train, grad_query, basis_out, prev, half_sum)
    given = [lax.ppermute(piece, "col", flip) for piece in give]
    prev = meet(1, keep)
    if line:
        prev = after_part(prev, got[2])
    prev = meet(2, pay(0, prev))
    outs = pieces_of(keep.shape[1], 2)
    wide, thin = add_part(keep, given, prev, outs)
    prev, bit = wide, 2
    while bit < n_col:
        other = [lax.ppermute(x, "col", [(d, d ^ bit) for d in range(n_col)]) for x in thin]
        if bit == 2:
            more, _ = in_part(act_train, act_query, basis_in, prev, chunks[early:], [])
            parts += more
            prev = meet(3, pay(1, more[-1]))
            invs = inverse_part(correction, prev, chunks)
            prev = pay(2, invs[0])
        wide, thin = add_part(wide, other, prev, outs)
        prev = wide
        bit *= 2
    other = [lax.ppermute(x, "col", flip) for x in thin]
    prev = meet(5, pay(3, meet(4, prev)))
    rot_gt, rot_gq_t = join_part(thin, other, prev, tokens)
    prev = rot_gt
    halves = n_row if n_row == 4 and n_col == 4 and tokens % (n_row * LANES) == 0 else 0
    sums = score(0, [rot_gt], prev)
    done = 1
    for j in range(6, count + 1):
        prev = meet(j, pay(j - 2, sums[0]))
        sums = score(done, sums, prev)
        done += 1
    if line:
        prev = after_part(sums[0], got[count])
    prev = pay(count - 1, prev)
    for k in range(done, count):
        sums = score(k, sums, prev)
    if not halves:
        blocks = sums[0].reshape(NQ, n_row, tokens // n_row).transpose(1, 0, 2)
        return shared_sum(owned_sum(blocks, "row"), "col")
    moved = [
        lax.ppermute(sums[step], "row", [(d, d ^ step) for d in range(n_row)])
        for step in range(1, n_row)
    ]
    owned = gather_part([sums[0]] + moved)
    moved = [
        lax.ppermute(owned, "col", [(d, d ^ step) for d in range(n_col)]) for step in range(1, n_col)
    ]
    return gather_part([owned] + moved)


def solution(mesh):
    in_specs = (
        P("groups", "row"),
        P("groups", "row"),
        P("groups", "col"),
        P("groups", "col"),
        P(("groups", "row"), "col"),
        P(("groups", "col"), "row"),
        P(("groups", "row"), "col"),
    )
    out_specs = P("groups", "row")
    return jax.shard_map(
        on_device, mesh=mesh, in_specs=in_specs, out_specs=out_specs, check_vma=False
    )
```

profile of v0, /device:TPU:1, one launch (start us, length us, event | category | flops | bytes accessed | tf_op | source)
XLA Modules:
  0.0 110.9 jit_solution(2826597418957463311)
XLA Ops:
  0.0 2.7 %shard_map.73 = (f32[640,256]{1,0:T(8,128)S(1)}, bf16[640,256]{1,0:T(8,128)(2,1)S(1)}) custom-call(bf16[512,2048]{1,0:T(8,128)(2,1)} %train_ref.9, bf16[128,2048]{1,0:T(8,128)(2,1)} %query_ref.9, bf16[2048,2048]{1,0:T(8,128)(2,1)} %basis_ref.9, bf16[128,2048]{1,0:T(8,128)(2,1)} %query_ref.9), custom_call_target="tpu_custom_call" | custom-call | flops 1024 | bytes 1024 | tf_op jit(solution)/shard_map/pallas_call | solution.py:116
  2.7 2.2 %collective-permute-start = (bf16[640,256]{1,0:T(8,128)(2,1)S(1)}, bf16[640,256]{1,0:T(8,128)(2,1)S(1)}, u32[]{:S(2)}, u32[]{:S(2)}) collective-permute-start(bf16[640,256]{1,0:T(8,128)(2,1)S(1)} %get-tuple-element.56), channel_id=1, source_target_pairs={{0,4},{4,0},{8,12},{12,8},{1,5},{5,1},{9,13},{13,9},{2,6},{6,2},{1... | collective-permute-start | bytes 983048 | tf_op jit(solution)/shard_map/ppermute | solution.py:525
  4.9 5.1 %shard_map.74 = (f32[640,256]{1,0:T(8,128)S(1)}, f32[640,256]{1,0:T(8,128)S(1)}, f32[640,256]{1,0:T(8,128)S(1)}, f32[640,256]{1,0:T(8,128)S(1)}, bf16[640,256]{1,0:T(8,128)(2,1)S(1)}) custom-call(bf16[512,2048]{1,0:T(8,128)(2,1)} %train_ref.9, bf16[128,2048]{1,0:T(8,128)(2,1)} %query_ref.9, bf16[2048,2048]{1,0:T(8,128)(2,1)} %basis_ref.9, ...), custom_call_target="tpu_custom_call" | custom-call | flops 1024 | bytes 1024 | tf_op jit(solution)/shard_map/pallas_call | solution.py:116
  10.1 5.0 %shard_map.75.refs_2_.refs_0_ = f32[640,1024]{1,0:T(8,128)S(1)} custom-call(bf16[512,7168]{1,0:T(8,128)(2,1)} %train_ref.8, bf16[128,7168]{1,0:T(8,128)(2,1)} %query_ref.8, bf16[7168,1024]{1,0:T(8,128)(2,1)} %basis_ref.8, f32[640,256]{1,0:T(8,128)S(1)} %get-tuple-element.58.prev_ref.refs_0_.keep_ref), custom_call_target="tpu_custom_call" | custom-call | flops 1024 | bytes 1024 | tf_op jit(solution)/shard_map/pallas_call | solution.py:204
  15.2 1.5 %collective-permute-start.3 = (bf16[640,256]{1,0:T(8,128)(2,1)S(1)}, bf16[640,256]{1,0:T(8,128)(2,1)S(1)}, u32[]{:S(2)}, u32[]{:S(2)}) collective-permute-start(bf16[640,256]{1,0:T(8,128)(2,1)S(1)} %get-tuple-element.63), channel_id=1, source_target_pairs={{0,4},{4,0},{8,12},{12,8},{1,5},{5,1},{9,13},{13,9},{2,6},{6,2},{1... | collective-permute-start | bytes 983048 | tf_op jit(solution)/shard_map/ppermute | solution.py:525
  16.8 1.5 %collective-permute-start.4 = (bf16[640,256]{1,0:T(8,128)(2,1)S(1)}, bf16[640,256]{1,0:T(8,128)(2,1)S(1)}, u32[]{:S(2)}, u32[]{:S(2)}) collective-permute-start(bf16[640,256]{1,0:T(8,128)(2,1)S(1)} %get-tuple-element.59.prev_ref), channel_id=1, source_target_pairs={{4,8},{8,4},{0,1},{12,13},{5,9},{9,5},{1,0},{13,12},{6,10},{10,6},... | collective-permute-start | bytes 983048 | tf_op jit(solution)/shard_map/ppermute | solution.py:532
  18.3 10.3 %shard_map.77 = (f32[320,1024]{1,0:T(8,128)S(1)}, f32[320,512]{1,0:T(8,128)S(1)}, f32[320,512]{1,0:T(8,128)S(1)}) custom-call(bf16[512,7168]{1,0:T(8,128)(2,1)} %train_ref.8, bf16[128,7168]{1,0:T(8,128)(2,1)} %query_ref.8, bf16[7168,1024]{1,0:T(8,128)(2,1)} %basis_ref.8, bf16[640,256]{1,0:T(8,128)(2,1)S(1)} %get-tuple-element.59.prev_ref, ...), custom_call_target="tpu_custom_call" | custom-call | flops 6710886400 | bytes 1024 | tf_op jit(solution)/shard_map/pallas_call | solution.py:204
  29.6 2.5 %collective-permute-start.7 = (bf16[640,256]{1,0:T(8,128)(2,1)S(1)}, bf16[640,256]{1,0:T(8,128)(2,1)S(1)}, u32[]{:S(2)}, u32[]{:S(2)}) collective-permute-start(bf16[640,256]{1,0:T(8,128)(2,1)S(1)} %shard_map.80.refs_1_.sent_ref), channel_id=1, source_target_pairs={{0,4},{4,0},{8,12},{12,8},{1,5},{5,1},{9,13},{13,9},{2,6},{6,2},{1... | collective-permute-start | bytes 983048 | tf_op jit(solution)/shard_map/ppermute | solution.py:525
  34.6 4.3 %shard_map.83 = (f32[640,256]{1,0:T(8,128)S(1)}, f32[640,256]{1,0:T(8,128)S(1)}, f32[640,256]{1,0:T(8,128)S(1)}) custom-call(bf16[512,2048]{1,0:T(8,128)(2,1)} %train_ref.9, bf16[128,2048]{1,0:T(8,128)(2,1)} %query_ref.9, bf16[2048,2048]{1,0:T(8,128)(2,1)} %basis_ref.9, f32[320,1024]{1,0:T(8,128)S(1)} %get-tuple-element.70.prev_ref.keep_ref), custom_call_target="tpu_custom_call" | custom-call | flops 1024 | bytes 1024 | tf_op jit(solution)/shard_map/pallas_call | solution.py:116
  39.0 1.8 %collective-permute-start.11 = (bf16[640,256]{1,0:T(8,128)(2,1)S(1)}, bf16[640,256]{1,0:T(8,128)(2,1)S(1)}, u32[]{:S(2)}, u32[]{:S(2)}) collective-permute-start(bf16[640,256]{1,0:T(8,128)(2,1)S(1)} %shard_map.84.refs_1_.sent_ref), channel_id=1, source_target_pairs={{0,4},{4,0},{8,12},{12,8},{1,5},{5,1},{9,13},{13,9},{2,6},{6,2},{1... | collective-permute-start | bytes 983048 | tf_op jit(solution)/shard_map/ppermute | solution.py:525
  40.9 2.5 %collective-permute-start.10 = (bf16[640,256]{1,0:T(8,128)(2,1)S(1)}, bf16[640,256]{1,0:T(8,128)(2,1)S(1)}, u32[]{:S(2)}, u32[]{:S(2)}) collective-permute-start(bf16[640,256]{1,0:T(8,128)(2,1)S(1)} %get-tuple-element.75.prev_ref), channel_id=1, source_target_pairs={{4,8},{8,4},{0,1},{12,13},{5,9},{9,5},{1,0},{13,12},{6,10},{10,6},... | collective-permute-start | bytes 983048 | tf_op jit(solution)/shard_map/ppermute | solution.py:532
  43.4 3.9 %shard_map.86 = (f32[1024,256]{1,0:T(8,128)S(1)}, f32[1024,256]{1,0:T(8,128)S(1)}, f32[1024,256]{1,0:T(8,128)S(1)}, f32[1024,256]{1,0:T(8,128)S(1)}, f32[1024,25...) custom-call(f32[1024,2048]{1,0:T(8,128)} %corr_ref.1, ...), custom_call_target="tpu_custom_call" | custom-call | flops 1024 | bytes 1024 | tf_op jit(solution)/shard_map/pallas_call | solution.py:325
  47.8 1.6 %collective-permute-done.13.refs_1_ = bf16[320,512]{1,0:T(8,128)(2,1)S(1)} collective-permute-done((bf16[320,512]{1,0:T(8,128)(2,1)S(1)}, bf16[320,512]{1,0:T(8,128)(2,1)S(1)}, u32[]{:S(2)}, u32[]{:S(2)}) %collective-permute-start.13) | collective-permute-done | bytes 327712 | tf_op jit(solution)/shard_map/ppermute | solution.py:577
  51.3 3.6 %collective-permute-start.19 = (bf16[640,256]{1,0:T(8,128)(2,1)S(1)}, bf16[640,256]{1,0:T(8,128)(2,1)S(1)}, u32[]{:S(2)}, u32[]{:S(2)}) collective-permute-start(bf16[640,256]{1,0:T(8,128)(2,1)S(1)} %shard_map.90.refs_1_.sent_ref), channel_id=1, source_target_pairs={{0,4},{4,0},{8,12},{12,8},{1,5},{5,1},{9,13},{13,9},{2,6},{6,2},{1... | collective-permute-start | bytes 983048 | tf_op jit(solution)/shard_map/ppermute | solution.py:525
  56.0 2.7 %collective-permute-start.18 = (bf16[640,256]{1,0:T(8,128)(2,1)S(1)}, bf16[640,256]{1,0:T(8,128)(2,1)S(1)}, u32[]{:S(2)}, u32[]{:S(2)}) collective-permute-start(bf16[640,256]{1,0:T(8,128)(2,1)S(1)} %get-tuple-element.83.prev_ref), channel_id=1, source_target_pairs={{4,8},{8,4},{0,1},{12,13},{5,9},{9,5},{1,0},{13,12},{6,10},{10,6},... | collective-permute-start | bytes 983048 | tf_op jit(solution)/shard_map/ppermute | solution.py:532
  59.2 3.5 %shard_map.93.refs_1_.prev_ref = f32[512,128]{1,0:T(8,128)S(1)} custom-call(bf16[512,1024]{1,0:T(8,128)(2,1)S(1)} %get-tuple-element.86.gt_ref.prev_ref.order_ref, bf16[1024,128]{1,0:T(8,128)(2,1)S(1)} %get-tuple-element.87.gq_ref, f32[1024,256]{1,0:T(8,128)S(1)} %get-tuple-element.76.refs_1_.inv_ref, bf16[640,256]{1,0:T(8,128)(2,1)S(1)} %shard_map.80.refs_1_.sent_ref, ...), custom_call_target="tpu_custom_call" | custom-call | flops 1024 | bytes 1024 | tf_op jit(solution)/shard_map/pallas_call | solution.py:438
  63.4 1.6 %collective-permute-start.21 = (bf16[640,256]{1,0:T(8,128)(2,1)S(1)}, bf16[640,256]{1,0:T(8,128)(2,1)S(1)}, u32[]{:S(2)}, u32[]{:S(2)}) collective-permute-start(bf16[640,256]{1,0:T(8,128)(2,1)S(1)} %get-tuple-element.92.order_ref), channel_id=1, source_target_pairs={{4,8},{8,4},{0,1},{12,13},{5,9},{9,5},{1,0},{13,12},{6,10},{10,6},... | collective-permute-start | bytes 983048 | tf_op jit(solution)/shard_map/ppermute | solution.py:532
  65.0 3.5 %shard_map.96.refs_0_.prev_ref = f32[512,128]{1,0:T(8,128)S(1)} custom-call(bf16[512,1024]{1,0:T(8,128)(2,1)S(1)} %get-tuple-element.86.gt_ref.prev_ref.order_ref, bf16[1024,128]{1,0:T(8,128)(2,1)S(1)} %get-tuple-element.87.gq_ref, f32[1024,256]{1,0:T(8,128)S(1)} %get-tuple-element.91.inv_ref, bf16[640,256]{1,0:T(8,128)(2,1)S(1)} %shard_map.84.refs_1_.sent_ref, ...), custom_call_target="tpu_custom_call" | custom-call | flops 1024 | bytes 1024 | tf_op jit(solution)/shard_map/pallas_call | solution.py:438
  69.1 3.2 %collective-permute-done.17.refs_0_.got_ref = bf16[640,256]{1,0:T(8,128)(2,1)S(1)} collective-permute-done((bf16[640,256]{1,0:T(8,128)(2,1)S(1)}, bf16[640,256]{1,0:T(8,128)(2,1)S(1)}, u32[]{:S(2)}, u32[]{:S(2)}) %collective-permute-start.17) | collective-permute-done | bytes 327712 | tf_op jit(solution)/shard_map/ppermute | solution.py:525
  72.3 1.3 %collective-permute-start.20 = (bf16[640,256]{1,0:T(8,128)(2,1)S(1)}, bf16[640,256]{1,0:T(8,128)(2,1)S(1)}, u32[]{:S(2)}, u32[]{:S(2)}) collective-permute-start(bf16[640,256]{1,0:T(8,128)(2,1)S(1)} %get-tuple-element.94.order_ref), channel_id=1, source_target_pairs={{4,8},{8,4},{0,1},{12,13},{5,9},{9,5},{1,0},{13,12},{6,10},{10,6},... | collective-permute-start | bytes 983048 | tf_op jit(solution)/shard_map/ppermute | solution.py:532
  73.6 3.5 %shard_map.99.refs_0_.prev_ref = f32[512,128]{1,0:T(8,128)S(1)} custom-call(bf16[512,1024]{1,0:T(8,128)(2,1)S(1)} %get-tuple-element.86.gt_ref.prev_ref.order_ref, bf16[1024,128]{1,0:T(8,128)(2,1)S(1)} %get-tuple-element.87.gq_ref, f32[1024,256]{1,0:T(8,128)S(1)} %get-tuple-element.96.inv_ref, bf16[640,256]{1,0:T(8,128)(2,1)S(1)} %shard_map.87.refs_2_.sent_ref, ...), custom_call_target="tpu_custom_call" | custom-call | flops 1024 | bytes 1024 | tf_op jit(solution)/shard_map/pallas_call | solution.py:438
  77.3 3.5 %shard_map.101.first_ref.prev_ref = f32[512,128]{1,0:T(8,128)S(1)} custom-call(bf16[512,1024]{1,0:T(8,128)(2,1)S(1)} %get-tuple-element.86.gt_ref.prev_ref.order_ref, bf16[1024,128]{1,0:T(8,128)(2,1)S(1)} %get-tuple-element.87.gq_ref, f32[1024,256]{1,0:T(8,128)S(1)} %get-tuple-element.95.inv_ref, bf16[640,256]{1,0:T(8,128)(2,1)S(1)} %shard_map.90.refs_1_.sent_ref, ...), custom_call_target="tpu_custom_call" | custom-call | flops 1024 | bytes 1024 | tf_op jit(solution)/shard_map/pallas_call | solution.py:438
  81.2 2.2 %collective-permute-start.23 = (bf16[640,256]{1,0:T(8,128)(2,1)S(1)}, bf16[640,256]{1,0:T(8,128)(2,1)S(1)}, u32[]{:S(2)}, u32[]{:S(2)}) collective-permute-start(bf16[640,256]{1,0:T(8,128)(2,1)S(1)} %shard_map.103.order_ref.sent_ref), channel_id=1, source_target_pairs={{0,4},{4,0},{8,12},{12,8},{1,5},{5,1},{9,13},{13,9},{2,6},{6,2},{1... | collective-permute-start | bytes 983048 | tf_op jit(solution)/shard_map/ppermute | solution.py:525
  83.3 3.5 %shard_map.104.prev_ref = f32[512,128]{1,0:T(8,128)S(1)} custom-call(bf16[512,1024]{1,0:T(8,128)(2,1)S(1)} %get-tuple-element.86.gt_ref.prev_ref.order_ref, bf16[1024,128]{1,0:T(8,128)(2,1)S(1)} %get-tuple-element.87.gq_ref, f32[1024,256]{1,0:T(8,128)S(1)} %get-tuple-element.100.inv_ref, bf16[640,256]{1,0:T(8,128)(2,1)S(1)} %shard_map.94.refs_1_.sent_ref, ...), custom_call_target="tpu_custom_call" | custom-call | flops 1024 | bytes 1024 | tf_op jit(solution)/shard_map/pallas_call | solution.py:438
  86.8 3.5 %shard_map.105.prev_ref = f32[512,128]{1,0:T(8,128)S(1)} custom-call(bf16[512,1024]{1,0:T(8,128)(2,1)S(1)} %get-tuple-element.86.gt_ref.prev_ref.order_ref, bf16[1024,128]{1,0:T(8,128)(2,1)S(1)} %get-tuple-element.87.gq_ref, f32[1024,256]{1,0:T(8,128)S(1)} %get-tuple-element.99.inv_ref, bf16[640,256]{1,0:T(8,128)(2,1)S(1)} %shard_map.97.refs_1_.sent_ref, ...), custom_call_target="tpu_custom_call" | custom-call | flops 1024 | bytes 1024 | tf_op jit(solution)/shard_map/pallas_call | solution.py:438
  90.4 3.5 %shard_map.106.prev_ref = f32[512,128]{1,0:T(8,128)S(1)} custom-call(bf16[512,1024]{1,0:T(8,128)(2,1)S(1)} %get-tuple-element.86.gt_ref.prev_ref.order_ref, bf16[1024,128]{1,0:T(8,128)(2,1)S(1)} %get-tuple-element.87.gq_ref, f32[1024,256]{1,0:T(8,128)S(1)} %get-tuple-element.98.inv_ref, bf16[640,256]{1,0:T(8,128)(2,1)S(1)} %shard_map.100.order_ref.sent_ref, ...), custom_call_target="tpu_custom_call" | custom-call | flops 1024 | bytes 1024 | tf_op jit(solution)/shard_map/pallas_call | solution.py:438
  93.9 3.6 %shard_map.107 = (f32[8,128]{1,0:T(8,128)S(1)}, f32[8,128]{1,0:T(8,128)S(1)}, f32[8,128]{1,0:T(8,128)S(1)}, f32[8,128]{1,0:T(8,128)S(1)}) custom-call(bf16[512,1024]{1,0:T(8,128)(2,1)S(1)} %get-tuple-element.86.gt_ref.prev_ref.order_ref, bf16[1024,128]{1,0:T(8,128)(2,1)S(1)} %get-tuple-element.87.gq_ref, f32[1024,256]{1,0:T(8,128)S(1)} %get-tuple-element.88.inv_ref, ...), custom_call_target="tpu_custom_call" | custom-call | flops 1024 | bytes 1024 | tf_op jit(solution)/shard_map/pallas_call | solution.py:438
  97.6 1.3 %collective-permute-start.26 = (f32[8,128]{1,0:T(8,128)S(1)}, f32[8,128]{1,0:T(8,128)S(1)}, u32[]{:S(2)}, u32[]{:S(2)}) collective-permute-start(f32[8,128]{1,0:T(8,128)S(1)} %get-tuple-element.103), channel_id=1, source_target_pairs={{0,8},{4,12},{8,0},{12,4},{1,9},{5,13},{9,1},{13,5},{2,10},{6,14},... | collective-permute-start | bytes 12296 | tf_op jit(solution)/shard_map/ppermute | solution.py:607
  98.9 2.2 %collective-permute-start.27 = (f32[8,128]{1,0:T(8,128)S(1)}, f32[8,128]{1,0:T(8,128)S(1)}, u32[]{:S(2)}, u32[]{:S(2)}) collective-permute-start(f32[8,128]{1,0:T(8,128)S(1)} %get-tuple-element.104), channel_id=1, source_target_pairs={{0,12},{4,8},{8,4},{12,0},{1,13},{5,9},{9,5},{13,1},{2,14},{6,10},... | collective-permute-start | bytes 12296 | tf_op jit(solution)/shard_map/ppermute | solution.py:607
  101.1 2.0 %collective-permute-done.27.refs_3_ = f32[8,128]{1,0:T(8,128)S(1)} collective-permute-done((f32[8,128]{1,0:T(8,128)S(1)}, f32[8,128]{1,0:T(8,128)S(1)}, u32[]{:S(2)}, u32[]{:S(2)}) %collective-permute-start.27) | collective-permute-done | bytes 4128 | tf_op jit(solution)/shard_map/ppermute | solution.py:607
  103.1 2.9 %collective-permute-start.28 = (f32[8,128]{1,0:T(8,128)S(1)}, f32[8,128]{1,0:T(8,128)S(1)}, u32[]{:S(2)}, u32[]{:S(2)}) collective-permute-start(f32[8,128]{1,0:T(8,128)S(1)} %shard_map.108.refs_0_), channel_id=1, source_target_pairs={{0,1},{1,0},{2,3},{3,2},{4,5},{5,4},{6,7},{7,6},{8,9},{9,8},{10,11... | collective-permute-start | bytes 12296 | tf_op jit(solution)/shard_map/ppermute | solution.py:612
  108.5 1.8 %collective-permute-done.30.refs_3_ = f32[8,128]{1,0:T(8,128)S(1)} collective-permute-done((f32[8,128]{1,0:T(8,128)S(1)}, f32[8,128]{1,0:T(8,128)S(1)}, u32[]{:S(2)}, u32[]{:S(2)}) %collective-permute-start.30) | collective-permute-done | bytes 4128 | tf_op jit(solution)/shard_map/ppermute | solution.py:612
  (67 shorter events, 12.7 us)
Async XLA Ops:
  2.7 12.4 %collective-permute-start = (bf16[640,256]{1,0:T(8,128)(2,1)S(1)}, bf16[640,256]{1,0:T(8,128)(2,1)S(1)}, u32[]{:S(2)}, u32[]{:S(2)}) collective-permute-start(bf16[640,256]{1,0:T(8,128)(2,1)S(1)} %get-tuple-element.56), channel_id=1, source_target_pairs={{0,4},{4,0},{8,12},{12,8},{1,5},{5,1},{9,13},{13,9},{2,6},{6,2},{1... | collective-permute-start | bytes 983048 | tf_op jit(solution)/shard_map/ppermute | solution.py:525
  10.0 19.2 %collective-permute-start.5 = (bf16[640,256]{1,0:T(8,128)(2,1)S(1)}, bf16[640,256]{1,0:T(8,128)(2,1)S(1)}, u32[]{:S(2)}, u32[]{:S(2)}) collective-permute-start(bf16[640,256]{1,0:T(8,128)(2,1)S(1)} %get-tuple-element.67), channel_id=1, source_target_pairs={{0,4},{4,0},{8,12},{12,8},{1,5},{5,1},{9,13},{13,9},{2,6},{6,2},{1... | collective-permute-start | bytes 983048 | tf_op jit(solution)/shard_map/ppermute | solution.py:525
  15.2 14.2 %collective-permute-start.3 = (bf16[640,256]{1,0:T(8,128)(2,1)S(1)}, bf16[640,256]{1,0:T(8,128)(2,1)S(1)}, u32[]{:S(2)}, u32[]{:S(2)}) collective-permute-start(bf16[640,256]{1,0:T(8,128)(2,1)S(1)} %get-tuple-element.63), channel_id=1, source_target_pairs={{0,4},{4,0},{8,12},{12,8},{1,5},{5,1},{9,13},{13,9},{2,6},{6,2},{1... | collective-permute-start | bytes 983048 | tf_op jit(solution)/shard_map/ppermute | solution.py:525
  16.8 12.7 %collective-permute-start.4 = (bf16[640,256]{1,0:T(8,128)(2,1)S(1)}, bf16[640,256]{1,0:T(8,128)(2,1)S(1)}, u32[]{:S(2)}, u32[]{:S(2)}) collective-permute-start(bf16[640,256]{1,0:T(8,128)(2,1)S(1)} %get-tuple-element.59.prev_ref), channel_id=1, source_target_pairs={{4,8},{8,4},{0,1},{12,13},{5,9},{9,5},{1,0},{13,12},{6,10},{10,6},... | collective-permute-start | bytes 983048 | tf_op jit(solution)/shard_map/ppermute | solution.py:532
  28.6 4.3 %collective-permute-start.1 = (f32[320,512]{1,0:T(8,128)S(1)}, f32[320,512]{1,0:T(8,128)S(1)}, u32[]{:S(2)}, u32[]{:S(2)}) collective-permute-start(f32[320,512]{1,0:T(8,128)S(1)} %get-tuple-element.61), channel_id=1, source_target_pairs={{0,1},{1,0},{2,3},{3,2},{4,5},{5,4},{6,7},{7,6},{8,9},{9,8},{10,11... | collective-permute-start | bytes 1966088 | tf_op jit(solution)/shard_map/ppermute | solution.py:568
  28.7 4.2 %collective-permute-start.2 = (f32[320,512]{1,0:T(8,128)S(1)}, f32[320,512]{1,0:T(8,128)S(1)}, u32[]{:S(2)}, u32[]{:S(2)}) collective-permute-start(f32[320,512]{1,0:T(8,128)S(1)} %get-tuple-element.62), channel_id=1, source_target_pairs={{0,1},{1,0},{2,3},{3,2},{4,5},{5,4},{6,7},{7,6},{8,9},{9,8},{10,11... | collective-permute-start | bytes 1966088 | tf_op jit(solution)/shard_map/ppermute | solution.py:568
  29.3 9.6 %collective-permute-start.8 = (bf16[640,256]{1,0:T(8,128)(2,1)S(1)}, bf16[640,256]{1,0:T(8,128)(2,1)S(1)}, u32[]{:S(2)}, u32[]{:S(2)}) collective-permute-start(bf16[640,256]{1,0:T(8,128)(2,1)S(1)} %get-tuple-element.68.first_ref), channel_id=1, source_target_pairs={{4,8},{8,4},{0,1},{12,13},{5,9},{9,5},{1,0},{13,12},{6,10},{10,6},... | collective-permute-start | bytes 983048 | tf_op jit(solution)/shard_map/ppermute | solution.py:532
  29.6 11.3 %collective-permute-start.7 = (bf16[640,256]{1,0:T(8,128)(2,1)S(1)}, bf16[640,256]{1,0:T(8,128)(2,1)S(1)}, u32[]{:S(2)}, u32[]{:S(2)}) collective-permute-start(bf16[640,256]{1,0:T(8,128)(2,1)S(1)} %shard_map.80.refs_1_.sent_ref), channel_id=1, source_target_pairs={{0,4},{4,0},{8,12},{12,8},{1,5},{5,1},{9,13},{13,9},{2,6},{6,2},{1... | collective-permute-start | bytes 983048 | tf_op jit(solution)/shard_map/ppermute | solution.py:525
  32.1 15.2 %collective-permute-start.6 = (bf16[640,256]{1,0:T(8,128)(2,1)S(1)}, bf16[640,256]{1,0:T(8,128)(2,1)S(1)}, u32[]{:S(2)}, u32[]{:S(2)}) collective-permute-start(bf16[640,256]{1,0:T(8,128)(2,1)S(1)} %get-tuple-element.69.refs_2_), channel_id=1, source_target_pairs={{4,8},{8,4},{0,1},{12,13},{5,9},{9,5},{1,0},{13,12},{6,10},{10,6},... | collective-permute-start | bytes 983048 | tf_op jit(solution)/shard_map/ppermute | solution.py:532
  33.1 14.8 %collective-permute-start.12 = (bf16[320,512]{1,0:T(8,128)(2,1)S(1)}, bf16[320,512]{1,0:T(8,128)(2,1)S(1)}, u32[]{:S(2)}, u32[]{:S(2)}) collective-permute-start(bf16[320,512]{1,0:T(8,128)(2,1)S(1)} %get-tuple-element.79), channel_id=1, source_target_pairs={{0,2},{1,3},{2,0},{3,1},{4,6},{5,7},{6,4},{7,5},{8,10},{9,11},{10,... | collective-permute-start | bytes 983048 | tf_op jit(solution)/shard_map/ppermute | solution.py:577
  34.4 15.1 %collective-permute-start.13 = (bf16[320,512]{1,0:T(8,128)(2,1)S(1)}, bf16[320,512]{1,0:T(8,128)(2,1)S(1)}, u32[]{:S(2)}, u32[]{:S(2)}) collective-permute-start(bf16[320,512]{1,0:T(8,128)(2,1)S(1)} %get-tuple-element.80), channel_id=1, source_target_pairs={{0,2},{1,3},{2,0},{3,1},{4,6},{5,7},{6,4},{7,5},{8,10},{9,11},{10,... | collective-permute-start | bytes 983048 | tf_op jit(solution)/shard_map/ppermute | solution.py:577
  39.0 11.6 %collective-permute-start.11 = (bf16[640,256]{1,0:T(8,128)(2,1)S(1)}, bf16[640,256]{1,0:T(8,128)(2,1)S(1)}, u32[]{:S(2)}, u32[]{:S(2)}) collective-permute-start(bf16[640,256]{1,0:T(8,128)(2,1)S(1)} %shard_map.84.refs_1_.sent_ref), channel_id=1, source_target_pairs={{0,4},{4,0},{8,12},{12,8},{1,5},{5,1},{9,13},{13,9},{2,6},{6,2},{1... | collective-permute-start | bytes 983048 | tf_op jit(solution)/shard_map/ppermute | solution.py:525
  40.9 10.3 %collective-permute-start.10 = (bf16[640,256]{1,0:T(8,128)(2,1)S(1)}, bf16[640,256]{1,0:T(8,128)(2,1)S(1)}, u32[]{:S(2)}, u32[]{:S(2)}) collective-permute-start(bf16[640,256]{1,0:T(8,128)(2,1)S(1)} %get-tuple-element.75.prev_ref), channel_id=1, source_target_pairs={{4,8},{8,4},{0,1},{12,13},{5,9},{9,5},{1,0},{13,12},{6,10},{10,6},... | collective-permute-start | bytes 983048 | tf_op jit(solution)/shard_map/ppermute | solution.py:532
  47.4 8.5 %collective-permute-start.9 = (bf16[640,256]{1,0:T(8,128)(2,1)S(1)}, bf16[640,256]{1,0:T(8,128)(2,1)S(1)}, u32[]{:S(2)}, u32[]{:S(2)}) collective-permute-start(bf16[640,256]{1,0:T(8,128)(2,1)S(1)} %shard_map.87.refs_2_.sent_ref), channel_id=1, source_target_pairs={{0,4},{4,0},{8,12},{12,8},{1,5},{5,1},{9,13},{13,9},{2,6},{6,2},{1... | collective-permute-start | bytes 983048 | tf_op jit(solution)/shard_map/ppermute | solution.py:525
  49.6 9.1 %collective-permute-start.14 = (bf16[320,512]{1,0:T(8,128)(2,1)S(1)}, bf16[320,512]{1,0:T(8,128)(2,1)S(1)}, u32[]{:S(2)}, u32[]{:S(2)}) collective-permute-start(bf16[320,512]{1,0:T(8,128)(2,1)S(1)} %get-tuple-element.84.refs_0_), channel_id=1, source_target_pairs={{0,1},{1,0},{2,3},{3,2},{4,5},{5,4},{6,7},{7,6},{8,9},{9,8},{10,11... | collective-permute-start | bytes 983048 | tf_op jit(solution)/shard_map/ppermute | solution.py:587
  50.5 8.2 %collective-permute-start.15 = (bf16[320,512]{1,0:T(8,128)(2,1)S(1)}, bf16[320,512]{1,0:T(8,128)(2,1)S(1)}, u32[]{:S(2)}, u32[]{:S(2)}) collective-permute-start(bf16[320,512]{1,0:T(8,128)(2,1)S(1)} %get-tuple-element.85.refs_1_), channel_id=1, source_target_pairs={{0,1},{1,0},{2,3},{3,2},{4,5},{5,4},{6,7},{7,6},{8,9},{9,8},{10,11... | collective-permute-start | bytes 983048 | tf_op jit(solution)/shard_map/ppermute | solution.py:587
  50.7 12.0 %collective-permute-start.16 = (bf16[640,256]{1,0:T(8,128)(2,1)S(1)}, bf16[640,256]{1,0:T(8,128)(2,1)S(1)}, u32[]{:S(2)}, u32[]{:S(2)}) collective-permute-start(bf16[640,256]{1,0:T(8,128)(2,1)S(1)} %get-tuple-element.82.refs_1_), channel_id=1, source_target_pairs={{4,8},{8,4},{0,1},{12,13},{5,9},{9,5},{1,0},{13,12},{6,10},{10,6},... | collective-permute-start | bytes 983048 | tf_op jit(solution)/shard_map/ppermute | solution.py:532
  51.3 11.8 %collective-permute-start.19 = (bf16[640,256]{1,0:T(8,128)(2,1)S(1)}, bf16[640,256]{1,0:T(8,128)(2,1)S(1)}, u32[]{:S(2)}, u32[]{:S(2)}) collective-permute-start(bf16[640,256]{1,0:T(8,128)(2,1)S(1)} %shard_map.90.refs_1_.sent_ref), channel_id=1, source_target_pairs={{0,4},{4,0},{8,12},{12,8},{1,5},{5,1},{9,13},{13,9},{2,6},{6,2},{1... | collective-permute-start | bytes 983048 | tf_op jit(solution)/shard_map/ppermute | solution.py:525
  56.0 12.4 %collective-permute-start.18 = (bf16[640,256]{1,0:T(8,128)(2,1)S(1)}, bf16[640,256]{1,0:T(8,128)(2,1)S(1)}, u32[]{:S(2)}, u32[]{:S(2)}) collective-permute-start(bf16[640,256]{1,0:T(8,128)(2,1)S(1)} %get-tuple-element.83.prev_ref), channel_id=1, source_target_pairs={{4,8},{8,4},{0,1},{12,13},{5,9},{9,5},{1,0},{13,12},{6,10},{10,6},... | collective-permute-start | bytes 983048 | tf_op jit(solution)/shard_map/ppermute | solution.py:532
  62.9 9.4 %collective-permute-start.17 = (bf16[640,256]{1,0:T(8,128)(2,1)S(1)}, bf16[640,256]{1,0:T(8,128)(2,1)S(1)}, u32[]{:S(2)}, u32[]{:S(2)}) collective-permute-start(bf16[640,256]{1,0:T(8,128)(2,1)S(1)} %shard_map.94.refs_1_.sent_ref), channel_id=1, source_target_pairs={{0,4},{4,0},{8,12},{12,8},{1,5},{5,1},{9,13},{13,9},{2,6},{6,2},{1... | collective-permute-start | bytes 983048 | tf_op jit(solution)/shard_map/ppermute | solution.py:525
  63.4 13.8 %collective-permute-start.21 = (bf16[640,256]{1,0:T(8,128)(2,1)S(1)}, bf16[640,256]{1,0:T(8,128)(2,1)S(1)}, u32[]{:S(2)}, u32[]{:S(2)}) collective-permute-start(bf16[640,256]{1,0:T(8,128)(2,1)S(1)} %get-tuple-element.92.order_ref), channel_id=1, source_target_pairs={{4,8},{8,4},{0,1},{12,13},{5,9},{9,5},{1,0},{13,12},{6,10},{10,6},... | collective-permute-start | bytes 983048 | tf_op jit(solution)/shard_map/ppermute | solution.py:532
  68.6 12.3 %collective-permute-start.22 = (bf16[640,256]{1,0:T(8,128)(2,1)S(1)}, bf16[640,256]{1,0:T(8,128)(2,1)S(1)}, u32[]{:S(2)}, u32[]{:S(2)}) collective-permute-start(bf16[640,256]{1,0:T(8,128)(2,1)S(1)} %shard_map.97.refs_1_.sent_ref), channel_id=1, source_target_pairs={{0,4},{4,0},{8,12},{12,8},{1,5},{5,1},{9,13},{13,9},{2,6},{6,2},{1... | collective-permute-start | bytes 983048 | tf_op jit(solution)/shard_map/ppermute | solution.py:525
  72.3 8.5 %collective-permute-start.20 = (bf16[640,256]{1,0:T(8,128)(2,1)S(1)}, bf16[640,256]{1,0:T(8,128)(2,1)S(1)}, u32[]{:S(2)}, u32[]{:S(2)}) collective-permute-start(bf16[640,256]{1,0:T(8,128)(2,1)S(1)} %get-tuple-element.94.order_ref), channel_id=1, source_target_pairs={{4,8},{8,4},{0,1},{12,13},{5,9},{9,5},{1,0},{13,12},{6,10},{10,6},... | collective-permute-start | bytes 983048 | tf_op jit(solution)/shard_map/ppermute | solution.py:532
  77.2 13.1 %collective-permute-start.24 = (bf16[640,256]{1,0:T(8,128)(2,1)S(1)}, bf16[640,256]{1,0:T(8,128)(2,1)S(1)}, u32[]{:S(2)}, u32[]{:S(2)}) collective-permute-start(bf16[640,256]{1,0:T(8,128)(2,1)S(1)} %shard_map.100.order_ref.sent_ref), channel_id=1, source_target_pairs={{0,4},{4,0},{8,12},{12,8},{1,5},{5,1},{9,13},{13,9},{2,6},{6,2},{1... | collective-permute-start | bytes 983048 | tf_op jit(solution)/shard_map/ppermute | solution.py:525
  81.2 12.7 %collective-permute-start.23 = (bf16[640,256]{1,0:T(8,128)(2,1)S(1)}, bf16[640,256]{1,0:T(8,128)(2,1)S(1)}, u32[]{:S(2)}, u32[]{:S(2)}) collective-permute-start(bf16[640,256]{1,0:T(8,128)(2,1)S(1)} %shard_map.103.order_ref.sent_ref), channel_id=1, source_target_pairs={{0,4},{4,0},{8,12},{12,8},{1,5},{5,1},{9,13},{13,9},{2,6},{6,2},{1... | collective-permute-start | bytes 983048 | tf_op jit(solution)/shard_map/ppermute | solution.py:525
  97.5 3.6 %collective-permute-start.25 = (f32[8,128]{1,0:T(8,128)S(1)}, f32[8,128]{1,0:T(8,128)S(1)}, u32[]{:S(2)}, u32[]{:S(2)}) collective-permute-start(f32[8,128]{1,0:T(8,128)S(1)} %get-tuple-element.102), channel_id=1, source_target_pairs={{0,4},{4,0},{8,12},{12,8},{1,5},{5,1},{9,13},{13,9},{2,6},{6,2},{1... | collective-permute-start | bytes 12296 | tf_op jit(solution)/shard_map/ppermute | solution.py:607
  97.6 3.5 %collective-permute-start.26 = (f32[8,128]{1,0:T(8,128)S(1)}, f32[8,128]{1,0:T(8,128)S(1)}, u32[]{:S(2)}, u32[]{:S(2)}) collective-permute-start(f32[8,128]{1,0:T(8,128)S(1)} %get-tuple-element.103), channel_id=1, source_target_pairs={{0,8},{4,12},{8,0},{12,4},{1,9},{5,13},{9,1},{13,5},{2,10},{6,14},... | collective-permute-start | bytes 12296 | tf_op jit(solution)/shard_map/ppermute | solution.py:607
  98.9 4.3 %collective-permute-start.27 = (f32[8,128]{1,0:T(8,128)S(1)}, f32[8,128]{1,0:T(8,128)S(1)}, u32[]{:S(2)}, u32[]{:S(2)}) collective-permute-start(f32[8,128]{1,0:T(8,128)S(1)} %get-tuple-element.104), channel_id=1, source_target_pairs={{0,12},{4,8},{8,4},{12,0},{1,13},{5,9},{9,5},{13,1},{2,14},{6,10},... | collective-permute-start | bytes 12296 | tf_op jit(solution)/shard_map/ppermute | solution.py:607
  103.1 4.7 %collective-permute-start.28 = (f32[8,128]{1,0:T(8,128)S(1)}, f32[8,128]{1,0:T(8,128)S(1)}, u32[]{:S(2)}, u32[]{:S(2)}) collective-permute-start(f32[8,128]{1,0:T(8,128)S(1)} %shard_map.108.refs_0_), channel_id=1, source_target_pairs={{0,1},{1,0},{2,3},{3,2},{4,5},{5,4},{6,7},{7,6},{8,9},{9,8},{10,11... | collective-permute-start | bytes 12296 | tf_op jit(solution)/shard_map/ppermute | solution.py:612
  106.1 2.5 %collective-permute-start.29 = (f32[8,128]{1,0:T(8,128)S(1)}, f32[8,128]{1,0:T(8,128)S(1)}, u32[]{:S(2)}, u32[]{:S(2)}) collective-permute-start(f32[8,128]{1,0:T(8,128)S(1)} %shard_map.108.refs_0_), channel_id=1, source_target_pairs={{0,2},{1,3},{2,0},{3,1},{4,6},{5,7},{6,4},{7,5},{8,10},{9,11},{10,... | collective-permute-start | bytes 12296 | tf_op jit(solution)/shard_map/ppermute | solution.py:612
  107.3 3.0 %collective-permute-start.30 = (f32[8,128]{1,0:T(8,128)S(1)}, f32[8,128]{1,0:T(8,128)S(1)}, u32[]{:S(2)}, u32[]{:S(2)}) collective-permute-start(f32[8,128]{1,0:T(8,128)S(1)} %shard_map.108.refs_0_), channel_id=1, source_target_pairs={{0,3},{1,2},{2,1},{3,0},{4,7},{5,6},{6,5},{7,4},{8,11},{9,10},{10,... | collective-permute-start | bytes 12296 | tf_op jit(solution)/shard_map/ppermute | solution.py:612
where the time goes:
time: 111 us
  Pallas kernels  62.7 us (56%)
  starting transfers between devices  37.2 us (34%)
  waiting for transfers between devices  10.7 us (10%)
    pallas_call x8, Pallas kernels, score_part(): pl.pallas_call(functools.partial(score_kernel, start, scale, len(out_shap...  28.2 us
    pallas_call x2, Pallas kernels, out_part(): pl.pallas_call(functools.partial(out_kernel, begin, count, last), in_spec...  15.4 us
    ppermute x11, starting transfers between devices, swap(): got[j] = lax.ppermute(payload, 'row', outer)  14.8 us
    pallas_call x3, Pallas kernels, in_part(): pl.pallas_call(functools.partial(in_kernel, chunks, len(narrow), groups),...  12.1 us
    ppermute x8, starting transfers between devices, meet(): got_mid[j] = lax.ppermute(thin[0], ('row', 'col'), inner)  11.1 us
    ppermute x3, starting transfers between devices, on_device(): lax.ppermute(owned, 'col', [(d, d ^ step) for d in range(n_col)])  4.65 us
    ppermute x11, waiting for transfers between devices, swap(): got[j] = lax.ppermute(payload, 'row', outer)  4.43 us
    pallas_call x1, Pallas kernels, inverse_part(): pl.pallas_call(functools.partial(inverse_kernel, chunks), in_specs=[ANY_S...  3.86 us
  transfers between devices with their start and end apart: 31, of which 7 were waited for; matrix products, arithmetic and copies ran while one was open for 0% of the time, Pallas kernels for 50%

commit v1 on v0

--- a/solution.py
+++ b/solution.py
@@ -87,16 +87,23 @@
     for g in range(groups):
         for copy in copies(g):
             copy.start()
-    sum_ref[...] = jnp.zeros_like(sum_ref)
 
     def body(g, carry):
         for copy in copies(g):
             copy.wait()
         for h, value in enumerate(halves_dot(rows_ref[g], slot_ref[g])):
-            sum_ref[h * half : (h + 1) * half, :] += value
+            span = slice(h * half, (h + 1) * half)
+            if isinstance(g, int):
+                sum_ref[span, :] = value + sum_ref[span, :] if g > 0 else value
+            else:
+                sum_ref[span, :] = value + jnp.where(g > 0, sum_ref[span, :], 0.0)
         return carry
 
-    lax.fori_loop(0, groups, body, 0)
+    if total <= 2 * LANES:
+        for g in range(groups):
+            body(g, 0)
+    else:
+        lax.fori_loop(0, groups, body, 0)
     for j, (first, width) in enumerate(chunks):
         refs[j][...] = sum_ref[:, first - start : first - start + width]
     column = 0

time: 111 us -> 111 us (level)
  no operation moved by 1% of the time
where the time goes in v1:
time: 111 us
  Pallas kernels  62.4 us (56%)
  starting transfers between devices  37.2 us (34%)
  waiting for transfers between devices  10.7 us (10%)
    pallas_call x8, Pallas kernels, score_part(): pl.pallas_call(functools.partial(score_kernel, start, scale, len(out_shap...  28.2 us
    pallas_call x2, Pallas kernels, out_part(): pl.pallas_call(functools.partial(out_kernel, begin, count, last), in_spec...  15.4 us
    ppermute x11, starting transfers between devices, swap(): got[j] = lax.ppermute(payload, 'row', outer)  14.9 us
    pallas_call x3, Pallas kernels, in_part(): pl.pallas_call(functools.partial(in_kernel, chunks, len(narrow), groups),...  11.8 us
    ppermute x8, starting transfers between devices, meet(): got_mid[j] = lax.ppermute(thin[0], ('row', 'col'), inner)  11 us
    ppermute x3, starting transfers between devices, on_device(): lax.ppermute(owned, 'col', [(d, d ^ step) for d in range(n_col)])  4.65 us
    ppermute x11, waiting for transfers between devices, swap(): got[j] = lax.ppermute(payload, 'row', outer)  4.44 us
    pallas_call x1, Pallas kernels, inverse_part(): pl.pallas_call(functools.partial(inverse_kernel, chunks), in_specs=[ANY_S...  3.86 us
  transfers between devices with their start and end apart: 31, of which 7 were waited for; matrix products, arithmetic and copies ran while one was open for 0% of the time, Pallas kernels for 50%

profile of v1, /device:TPU:1, one launch (start us, length us, event | category | flops | bytes accessed | tf_op | source)
XLA Modules:
  0.0 110.7 jit_solution(4235722098720691160)
XLA Ops:
  0.0 2.4 %shard_map.73 = (f32[640,256]{1,0:T(8,128)S(1)}, bf16[640,256]{1,0:T(8,128)(2,1)S(1)}) custom-call(bf16[512,2048]{1,0:T(8,128)(2,1)} %train_ref.9, bf16[128,2048]{1,0:T(8,128)(2,1)} %query_ref.9, bf16[2048,2048]{1,0:T(8,128)(2,1)} %basis_ref.9, bf16[128,2048]{1,0:T(8,128)(2,1)} %query_ref.9), custom_call_target="tpu_custom_call" | custom-call | flops 1024 | bytes 1024 | tf_op jit(solution)/shard_map/pallas_call | solution.py:123
  2.5 2.2 %collective-permute-start = (bf16[640,256]{1,0:T(8,128)(2,1)S(1)}, bf16[640,256]{1,0:T(8,128)(2,1)S(1)}, u32[]{:S(2)}, u32[]{:S(2)}) collective-permute-start(bf16[640,256]{1,0:T(8,128)(2,1)S(1)} %get-tuple-element.56), channel_id=1, source_target_pairs={{0,4},{4,0},{8,12},{12,8},{1,5},{5,1},{9,13},{13,9},{2,6},{6,2},{1... | collective-permute-start | bytes 983048 | tf_op jit(solution)/shard_map/ppermute | solution.py:532
  4.6 5.1 %shard_map.74 = (f32[640,256]{1,0:T(8,128)S(1)}, f32[640,256]{1,0:T(8,128)S(1)}, f32[640,256]{1,0:T(8,128)S(1)}, f32[640,256]{1,0:T(8,128)S(1)}, bf16[640,256]{1,0:T(8,128)(2,1)S(1)}) custom-call(bf16[512,2048]{1,0:T(8,128)(2,1)} %train_ref.9, bf16[128,2048]{1,0:T(8,128)(2,1)} %query_ref.9, bf16[2048,2048]{1,0:T(8,128)(2,1)} %basis_ref.9, ...), custom_call_target="tpu_custom_call" | custom-call | flops 1024 | bytes 1024 | tf_op jit(solution)/shard_map/pallas_call | solution.py:123
  9.9 5.0 %shard_map.75.refs_2_.refs_0_ = f32[640,1024]{1,0:T(8,128)S(1)} custom-call(bf16[512,7168]{1,0:T(8,128)(2,1)} %train_ref.8, bf16[128,7168]{1,0:T(8,128)(2,1)} %query_ref.8, bf16[7168,1024]{1,0:T(8,128)(2,1)} %basis_ref.8, f32[640,256]{1,0:T(8,128)S(1)} %get-tuple-element.58.prev_ref.refs_0_.keep_ref), custom_call_target="tpu_custom_call" | custom-call | flops 1024 | bytes 1024 | tf_op jit(solution)/shard_map/pallas_call | solution.py:211
  15.0 1.5 %collective-permute-start.3 = (bf16[640,256]{1,0:T(8,128)(2,1)S(1)}, bf16[640,256]{1,0:T(8,128)(2,1)S(1)}, u32[]{:S(2)}, u32[]{:S(2)}) collective-permute-start(bf16[640,256]{1,0:T(8,128)(2,1)S(1)} %get-tuple-element.63), channel_id=1, source_target_pairs={{0,4},{4,0},{8,12},{12,8},{1,5},{5,1},{9,13},{13,9},{2,6},{6,2},{1... | collective-permute-start | bytes 983048 | tf_op jit(solution)/shard_map/ppermute | solution.py:532
  16.5 1.5 %collective-permute-start.4 = (bf16[640,256]{1,0:T(8,128)(2,1)S(1)}, bf16[640,256]{1,0:T(8,128)(2,1)S(1)}, u32[]{:S(2)}, u32[]{:S(2)}) collective-permute-start(bf16[640,256]{1,0:T(8,128)(2,1)S(1)} %get-tuple-element.59.prev_ref), channel_id=1, source_target_pairs={{4,8},{8,4},{0,1},{12,13},{5,9},{9,5},{1,0},{13,12},{6,10},{10,6},... | collective-permute-start | bytes 983048 | tf_op jit(solution)/shard_map/ppermute | solution.py:539
  18.0 10.3 %shard_map.77 = (f32[320,1024]{1,0:T(8,128)S(1)}, f32[320,512]{1,0:T(8,128)S(1)}, f32[320,512]{1,0:T(8,128)S(1)}) custom-call(bf16[512,7168]{1,0:T(8,128)(2,1)} %train_ref.8, bf16[128,7168]{1,0:T(8,128)(2,1)} %query_ref.8, bf16[7168,1024]{1,0:T(8,128)(2,1)} %basis_ref.8, bf16[640,256]{1,0:T(8,128)(2,1)S(1)} %get-tuple-element.59.prev_ref, ...), custom_call_target="tpu_custom_call" | custom-call | flops 6710886400 | bytes 1024 | tf_op jit(solution)/shard_map/pallas_call | solution.py:211
  29.3 2.5 %collective-permute-start.7 = (bf16[640,256]{1,0:T(8,128)(2,1)S(1)}, bf16[640,256]{1,0:T(8,128)(2,1)S(1)}, u32[]{:S(2)}, u32[]{:S(2)}) collective-permute-start(bf16[640,256]{1,0:T(8,128)(2,1)S(1)} %shard_map.80.refs_1_.sent_ref), channel_id=1, source_target_pairs={{0,4},{4,0},{8,12},{12,8},{1,5},{5,1},{9,13},{13,9},{2,6},{6,2},{1... | collective-permute-start | bytes 983048 | tf_op jit(solution)/shard_map/ppermute | solution.py:532
  34.4 4.3 %shard_map.83 = (f32[640,256]{1,0:T(8,128)S(1)}, f32[640,256]{1,0:T(8,128)S(1)}, f32[640,256]{1,0:T(8,128)S(1)}) custom-call(bf16[512,2048]{1,0:T(8,128)(2,1)} %train_ref.9, bf16[128,2048]{1,0:T(8,128)(2,1)} %query_ref.9, bf16[2048,2048]{1,0:T(8,128)(2,1)} %basis_ref.9, f32[320,1024]{1,0:T(8,128)S(1)} %get-tuple-element.70.prev_ref.keep_ref), custom_call_target="tpu_custom_call" | custom-call | flops 1024 | bytes 1024 | tf_op jit(solution)/shard_map/pallas_call | solution.py:123
  38.8 1.8 %collective-permute-start.11 = (bf16[640,256]{1,0:T(8,128)(2,1)S(1)}, bf16[640,256]{1,0:T(8,128)(2,1)S(1)}, u32[]{:S(2)}, u32[]{:S(2)}) collective-permute-start(bf16[640,256]{1,0:T(8,128)(2,1)S(1)} %shard_map.84.refs_1_.sent_ref), channel_id=1, source_target_pairs={{0,4},{4,0},{8,12},{12,8},{1,5},{5,1},{9,13},{13,9},{2,6},{6,2},{1... | collective-permute-start | bytes 983048 | tf_op jit(solution)/shard_map/ppermute | solution.py:532
  40.7 2.5 %collective-permute-start.10 = (bf16[640,256]{1,0:T(8,128)(2,1)S(1)}, bf16[640,256]{1,0:T(8,128)(2,1)S(1)}, u32[]{:S(2)}, u32[]{:S(2)}) collective-permute-start(bf16[640,256]{1,0:T(8,128)(2,1)S(1)} %get-tuple-element.75.prev_ref), channel_id=1, source_target_pairs={{4,8},{8,4},{0,1},{12,13},{5,9},{9,5},{1,0},{13,12},{6,10},{10,6},... | collective-permute-start | bytes 983048 | tf_op jit(solution)/shard_map/ppermute | solution.py:539
  43.2 3.9 %shard_map.86 = (f32[1024,256]{1,0:T(8,128)S(1)}, f32[1024,256]{1,0:T(8,128)S(1)}, f32[1024,256]{1,0:T(8,128)S(1)}, f32[1024,256]{1,0:T(8,128)S(1)}, f32[1024,25...) custom-call(f32[1024,2048]{1,0:T(8,128)} %corr_ref.1, ...), custom_call_target="tpu_custom_call" | custom-call | flops 1024 | bytes 1024 | tf_op jit(solution)/shard_map/pallas_call | solution.py:332
  47.6 1.6 %collective-permute-done.13.refs_1_ = bf16[320,512]{1,0:T(8,128)(2,1)S(1)} collective-permute-done((bf16[320,512]{1,0:T(8,128)(2,1)S(1)}, bf16[320,512]{1,0:T(8,128)(2,1)S(1)}, u32[]{:S(2)}, u32[]{:S(2)}) %collective-permute-start.13) | collective-permute-done | bytes 327712 | tf_op jit(solution)/shard_map/ppermute | solution.py:584
  51.1 3.6 %collective-permute-start.19 = (bf16[640,256]{1,0:T(8,128)(2,1)S(1)}, bf16[640,256]{1,0:T(8,128)(2,1)S(1)}, u32[]{:S(2)}, u32[]{:S(2)}) collective-permute-start(bf16[640,256]{1,0:T(8,128)(2,1)S(1)} %shard_map.90.refs_1_.sent_ref), channel_id=1, source_target_pairs={{0,4},{4,0},{8,12},{12,8},{1,5},{5,1},{9,13},{13,9},{2,6},{6,2},{1... | collective-permute-start | bytes 983048 | tf_op jit(solution)/shard_map/ppermute | solution.py:532
  55.8 2.7 %collective-permute-start.18 = (bf16[640,256]{1,0:T(8,128)(2,1)S(1)}, bf16[640,256]{1,0:T(8,128)(2,1)S(1)}, u32[]{:S(2)}, u32[]{:S(2)}) collective-permute-start(bf16[640,256]{1,0:T(8,128)(2,1)S(1)} %get-tuple-element.83.prev_ref), channel_id=1, source_target_pairs={{4,8},{8,4},{0,1},{12,13},{5,9},{9,5},{1,0},{13,12},{6,10},{10,6},... | collective-permute-start | bytes 983048 | tf_op jit(solution)/shard_map/ppermute | solution.py:539
  59.0 3.5 %shard_map.93.refs_1_.prev_ref = f32[512,128]{1,0:T(8,128)S(1)} custom-call(bf16[512,1024]{1,0:T(8,128)(2,1)S(1)} %get-tuple-element.86.gt_ref.prev_ref.order_ref, bf16[1024,128]{1,0:T(8,128)(2,1)S(1)} %get-tuple-element.87.gq_ref, f32[1024,256]{1,0:T(8,128)S(1)} %get-tuple-element.76.refs_1_.inv_ref, bf16[640,256]{1,0:T(8,128)(2,1)S(1)} %shard_map.80.refs_1_.sent_ref, ...), custom_call_target="tpu_custom_call" | custom-call | flops 1024 | bytes 1024 | tf_op jit(solution)/shard_map/pallas_call | solution.py:445
  63.1 1.6 %collective-permute-start.21 = (bf16[640,256]{1,0:T(8,128)(2,1)S(1)}, bf16[640,256]{1,0:T(8,128)(2,1)S(1)}, u32[]{:S(2)}, u32[]{:S(2)}) collective-permute-start(bf16[640,256]{1,0:T(8,128)(2,1)S(1)} %get-tuple-element.92.order_ref), channel_id=1, source_target_pairs={{4,8},{8,4},{0,1},{12,13},{5,9},{9,5},{1,0},{13,12},{6,10},{10,6},... | collective-permute-start | bytes 983048 | tf_op jit(solution)/shard_map/ppermute | solution.py:539
  64.7 3.5 %shard_map.96.refs_0_.prev_ref = f32[512,128]{1,0:T(8,128)S(1)} custom-call(bf16[512,1024]{1,0:T(8,128)(2,1)S(1)} %get-tuple-element.86.gt_ref.prev_ref.order_ref, bf16[1024,128]{1,0:T(8,128)(2,1)S(1)} %get-tuple-element.87.gq_ref, f32[1024,256]{1,0:T(8,128)S(1)} %get-tuple-element.91.inv_ref, bf16[640,256]{1,0:T(8,128)(2,1)S(1)} %shard_map.84.refs_1_.sent_ref, ...), custom_call_target="tpu_custom_call" | custom-call | flops 1024 | bytes 1024 | tf_op jit(solution)/shard_map/pallas_call | solution.py:445
  68.8 3.2 %collective-permute-done.17.refs_0_.got_ref = bf16[640,256]{1,0:T(8,128)(2,1)S(1)} collective-permute-done((bf16[640,256]{1,0:T(8,128)(2,1)S(1)}, bf16[640,256]{1,0:T(8,128)(2,1)S(1)}, u32[]{:S(2)}, u32[]{:S(2)}) %collective-permute-start.17) | collective-permute-done | bytes 327712 | tf_op jit(solution)/shard_map/ppermute | solution.py:532
  72.1 1.3 %collective-permute-start.20 = (bf16[640,256]{1,0:T(8,128)(2,1)S(1)}, bf16[640,256]{1,0:T(8,128)(2,1)S(1)}, u32[]{:S(2)}, u32[]{:S(2)}) collective-permute-start(bf16[640,256]{1,0:T(8,128)(2,1)S(1)} %get-tuple-element.94.order_ref), channel_id=1, source_target_pairs={{4,8},{8,4},{0,1},{12,13},{5,9},{9,5},{1,0},{13,12},{6,10},{10,6},... | collective-permute-start | bytes 983048 | tf_op jit(solution)/shard_map/ppermute | solution.py:539
  73.4 3.5 %shard_map.99.refs_0_.prev_ref = f32[512,128]{1,0:T(8,128)S(1)} custom-call(bf16[512,1024]{1,0:T(8,128)(2,1)S(1)} %get-tuple-element.86.gt_ref.prev_ref.order_ref, bf16[1024,128]{1,0:T(8,128)(2,1)S(1)} %get-tuple-element.87.gq_ref, f32[1024,256]{1,0:T(8,128)S(1)} %get-tuple-element.96.inv_ref, bf16[640,256]{1,0:T(8,128)(2,1)S(1)} %shard_map.87.refs_2_.sent_ref, ...), custom_call_target="tpu_custom_call" | custom-call | flops 1024 | bytes 1024 | tf_op jit(solution)/shard_map/pallas_call | solution.py:445
  77.1 3.5 %shard_map.101.first_ref.prev_ref = f32[512,128]{1,0:T(8,128)S(1)} custom-call(bf16[512,1024]{1,0:T(8,128)(2,1)S(1)} %get-tuple-element.86.gt_ref.prev_ref.order_ref, bf16[1024,128]{1,0:T(8,128)(2,1)S(1)} %get-tuple-element.87.gq_ref, f32[1024,256]{1,0:T(8,128)S(1)} %get-tuple-element.95.inv_ref, bf16[640,256]{1,0:T(8,128)(2,1)S(1)} %shard_map.90.refs_1_.sent_ref, ...), custom_call_target="tpu_custom_call" | custom-call | flops 1024 | bytes 1024 | tf_op jit(solution)/shard_map/pallas_call | solution.py:445
  80.9 2.2 %collective-permute-start.23 = (bf16[640,256]{1,0:T(8,128)(2,1)S(1)}, bf16[640,256]{1,0:T(8,128)(2,1)S(1)}, u32[]{:S(2)}, u32[]{:S(2)}) collective-permute-start(bf16[640,256]{1,0:T(8,128)(2,1)S(1)} %shard_map.103.order_ref.sent_ref), channel_id=1, source_target_pairs={{0,4},{4,0},{8,12},{12,8},{1,5},{5,1},{9,13},{13,9},{2,6},{6,2},{1... | collective-permute-start | bytes 983048 | tf_op jit(solution)/shard_map/ppermute | solution.py:532
  83.1 3.5 %shard_map.104.prev_ref = f32[512,128]{1,0:T(8,128)S(1)} custom-call(bf16[512,1024]{1,0:T(8,128)(2,1)S(1)} %get-tuple-element.86.gt_ref.prev_ref.order_ref, bf16[1024,128]{1,0:T(8,128)(2,1)S(1)} %get-tuple-element.87.gq_ref, f32[1024,256]{1,0:T(8,128)S(1)} %get-tuple-element.100.inv_ref, bf16[640,256]{1,0:T(8,128)(2,1)S(1)} %shard_map.94.refs_1_.sent_ref, ...), custom_call_target="tpu_custom_call" | custom-call | flops 1024 | bytes 1024 | tf_op jit(solution)/shard_map/pallas_call | solution.py:445
  86.6 3.5 %shard_map.105.prev_ref = f32[512,128]{1,0:T(8,128)S(1)} custom-call(bf16[512,1024]{1,0:T(8,128)(2,1)S(1)} %get-tuple-element.86.gt_ref.prev_ref.order_ref, bf16[1024,128]{1,0:T(8,128)(2,1)S(1)} %get-tuple-element.87.gq_ref, f32[1024,256]{1,0:T(8,128)S(1)} %get-tuple-element.99.inv_ref, bf16[640,256]{1,0:T(8,128)(2,1)S(1)} %shard_map.97.refs_1_.sent_ref, ...), custom_call_target="tpu_custom_call" | custom-call | flops 1024 | bytes 1024 | tf_op jit(solution)/shard_map/pallas_call | solution.py:445
  90.1 3.5 %shard_map.106.prev_ref = f32[512,128]{1,0:T(8,128)S(1)} custom-call(bf16[512,1024]{1,0:T(8,128)(2,1)S(1)} %get-tuple-element.86.gt_ref.prev_ref.order_ref, bf16[1024,128]{1,0:T(8,128)(2,1)S(1)} %get-tuple-element.87.gq_ref, f32[1024,256]{1,0:T(8,128)S(1)} %get-tuple-element.98.inv_ref, bf16[640,256]{1,0:T(8,128)(2,1)S(1)} %shard_map.100.order_ref.sent_ref, ...), custom_call_target="tpu_custom_call" | custom-call | flops 1024 | bytes 1024 | tf_op jit(solution)/shard_map/pallas_call | solution.py:445
  93.7 3.6 %shard_map.107 = (f32[8,128]{1,0:T(8,128)S(1)}, f32[8,128]{1,0:T(8,128)S(1)}, f32[8,128]{1,0:T(8,128)S(1)}, f32[8,128]{1,0:T(8,128)S(1)}) custom-call(bf16[512,1024]{1,0:T(8,128)(2,1)S(1)} %get-tuple-element.86.gt_ref.prev_ref.order_ref, bf16[1024,128]{1,0:T(8,128)(2,1)S(1)} %get-tuple-element.87.gq_ref, f32[1024,256]{1,0:T(8,128)S(1)} %get-tuple-element.88.inv_ref, ...), custom_call_target="tpu_custom_call" | custom-call | flops 1024 | bytes 1024 | tf_op jit(solution)/shard_map/pallas_call | solution.py:445
  97.3 1.3 %collective-permute-start.26 = (f32[8,128]{1,0:T(8,128)S(1)}, f32[8,128]{1,0:T(8,128)S(1)}, u32[]{:S(2)}, u32[]{:S(2)}) collective-permute-start(f32[8,128]{1,0:T(8,128)S(1)} %get-tuple-element.103), channel_id=1, source_target_pairs={{0,8},{4,12},{8,0},{12,4},{1,9},{5,13},{9,1},{13,5},{2,10},{6,14},... | collective-permute-start | bytes 12296 | tf_op jit(solution)/shard_map/ppermute | solution.py:614
  98.7 2.2 %collective-permute-start.27 = (f32[8,128]{1,0:T(8,128)S(1)}, f32[8,128]{1,0:T(8,128)S(1)}, u32[]{:S(2)}, u32[]{:S(2)}) collective-permute-start(f32[8,128]{1,0:T(8,128)S(1)} %get-tuple-element.104), channel_id=1, source_target_pairs={{0,12},{4,8},{8,4},{12,0},{1,13},{5,9},{9,5},{13,1},{2,14},{6,10},... | collective-permute-start | bytes 12296 | tf_op jit(solution)/shard_map/ppermute | solution.py:614
  100.9 2.0 %collective-permute-done.27.refs_3_ = f32[8,128]{1,0:T(8,128)S(1)} collective-permute-done((f32[8,128]{1,0:T(8,128)S(1)}, f32[8,128]{1,0:T(8,128)S(1)}, u32[]{:S(2)}, u32[]{:S(2)}) %collective-permute-start.27) | collective-permute-done | bytes 4128 | tf_op jit(solution)/shard_map/ppermute | solution.py:614
  102.9 2.9 %collective-permute-start.28 = (f32[8,128]{1,0:T(8,128)S(1)}, f32[8,128]{1,0:T(8,128)S(1)}, u32[]{:S(2)}, u32[]{:S(2)}) collective-permute-start(f32[8,128]{1,0:T(8,128)S(1)} %shard_map.108.refs_0_), channel_id=1, source_target_pairs={{0,1},{1,0},{2,3},{3,2},{4,5},{5,4},{6,7},{7,6},{8,9},{9,8},{10,11... | collective-permute-start | bytes 12296 | tf_op jit(solution)/shard_map/ppermute | solution.py:619
  108.3 1.8 %collective-permute-done.30.refs_3_ = f32[8,128]{1,0:T(8,128)S(1)} collective-permute-done((f32[8,128]{1,0:T(8,128)S(1)}, f32[8,128]{1,0:T(8,128)S(1)}, u32[]{:S(2)}, u32[]{:S(2)}) %collective-permute-start.30) | collective-permute-done | bytes 4128 | tf_op jit(solution)/shard_map/ppermute | solution.py:619
  (67 shorter events, 12.7 us)
Async XLA Ops:
  2.5 12.4 %collective-permute-start = (bf16[640,256]{1,0:T(8,128)(2,1)S(1)}, bf16[640,256]{1,0:T(8,128)(2,1)S(1)}, u32[]{:S(2)}, u32[]{:S(2)}) collective-permute-start(bf16[640,256]{1,0:T(8,128)(2,1)S(1)} %get-tuple-element.56), channel_id=1, source_target_pairs={{0,4},{4,0},{8,12},{12,8},{1,5},{5,1},{9,13},{13,9},{2,6},{6,2},{1... | collective-permute-start | bytes 983048 | tf_op jit(solution)/shard_map/ppermute | solution.py:532
  9.8 19.2 %collective-permute-start.5 = (bf16[640,256]{1,0:T(8,128)(2,1)S(1)}, bf16[640,256]{1,0:T(8,128)(2,1)S(1)}, u32[]{:S(2)}, u32[]{:S(2)}) collective-permute-start(bf16[640,256]{1,0:T(8,128)(2,1)S(1)} %get-tuple-element.67), channel_id=1, source_target_pairs={{0,4},{4,0},{8,12},{12,8},{1,5},{5,1},{9,13},{13,9},{2,6},{6,2},{1... | collective-permute-start | bytes 983048 | tf_op jit(solution)/shard_map/ppermute | solution.py:532
  15.0 14.2 %collective-permute-start.3 = (bf16[640,256]{1,0:T(8,128)(2,1)S(1)}, bf16[640,256]{1,0:T(8,128)(2,1)S(1)}, u32[]{:S(2)}, u32[]{:S(2)}) collective-permute-start(bf16[640,256]{1,0:T(8,128)(2,1)S(1)} %get-tuple-element.63), channel_id=1, source_target_pairs={{0,4},{4,0},{8,12},{12,8},{1,5},{5,1},{9,13},{13,9},{2,6},{6,2},{1... | collective-permute-start | bytes 983048 | tf_op jit(solution)/shard_map/ppermute | solution.py:532
  16.5 12.7 %collective-permute-start.4 = (bf16[640,256]{1,0:T(8,128)(2,1)S(1)}, bf16[640,256]{1,0:T(8,128)(2,1)S(1)}, u32[]{:S(2)}, u32[]{:S(2)}) collective-permute-start(bf16[640,256]{1,0:T(8,128)(2,1)S(1)} %get-tuple-element.59.prev_ref), channel_id=1, source_target_pairs={{4,8},{8,4},{0,1},{12,13},{5,9},{9,5},{1,0},{13,12},{6,10},{10,6},... | collective-permute-start | bytes 983048 | tf_op jit(solution)/shard_map/ppermute | solution.py:539
  28.4 4.3 %collective-permute-start.1 = (f32[320,512]{1,0:T(8,128)S(1)}, f32[320,512]{1,0:T(8,128)S(1)}, u32[]{:S(2)}, u32[]{:S(2)}) collective-permute-start(f32[320,512]{1,0:T(8,128)S(1)} %get-tuple-element.61), channel_id=1, source_target_pairs={{0,1},{1,0},{2,3},{3,2},{4,5},{5,4},{6,7},{7,6},{8,9},{9,8},{10,11... | collective-permute-start | bytes 1966088 | tf_op jit(solution)/shard_map/ppermute | solution.py:575
  28.5 4.2 %collective-permute-start.2 = (f32[320,512]{1,0:T(8,128)S(1)}, f32[320,512]{1,0:T(8,128)S(1)}, u32[]{:S(2)}, u32[]{:S(2)}) collective-permute-start(f32[320,512]{1,0:T(8,128)S(1)} %get-tuple-element.62), channel_id=1, source_target_pairs={{0,1},{1,0},{2,3},{3,2},{4,5},{5,4},{6,7},{7,6},{8,9},{9,8},{10,11... | collective-permute-start | bytes 1966088 | tf_op jit(solution)/shard_map/ppermute | solution.py:575
  29.1 9.6 %collective-permute-start.8 = (bf16[640,256]{1,0:T(8,128)(2,1)S(1)}, bf16[640,256]{1,0:T(8,128)(2,1)S(1)}, u32[]{:S(2)}, u32[]{:S(2)}) collective-permute-start(bf16[640,256]{1,0:T(8,128)(2,1)S(1)} %get-tuple-element.68.first_ref), channel_id=1, source_target_pairs={{4,8},{8,4},{0,1},{12,13},{5,9},{9,5},{1,0},{13,12},{6,10},{10,6},... | collective-permute-start | bytes 983048 | tf_op jit(solution)/shard_map/ppermute | solution.py:539
  29.3 11.3 %collective-permute-start.7 = (bf16[640,256]{1,0:T(8,128)(2,1)S(1)}, bf16[640,256]{1,0:T(8,128)(2,1)S(1)}, u32[]{:S(2)}, u32[]{:S(2)}) collective-permute-start(bf16[640,256]{1,0:T(8,128)(2,1)S(1)} %shard_map.80.refs_1_.sent_ref), channel_id=1, source_target_pairs={{0,4},{4,0},{8,12},{12,8},{1,5},{5,1},{9,13},{13,9},{2,6},{6,2},{1... | collective-permute-start | bytes 983048 | tf_op jit(solution)/shard_map/ppermute | solution.py:532
  31.9 15.2 %collective-permute-start.6 = (bf16[640,256]{1,0:T(8,128)(2,1)S(1)}, bf16[640,256]{1,0:T(8,128)(2,1)S(1)}, u32[]{:S(2)}, u32[]{:S(2)}) collective-permute-start(bf16[640,256]{1,0:T(8,128)(2,1)S(1)} %get-tuple-element.69.refs_2_), channel_id=1, source_target_pairs={{4,8},{8,4},{0,1},{12,13},{5,9},{9,5},{1,0},{13,12},{6,10},{10,6},... | collective-permute-start | bytes 983048 | tf_op jit(solution)/shard_map/ppermute | solution.py:539
  32.8 14.8 %collective-permute-start.12 = (bf16[320,512]{1,0:T(8,128)(2,1)S(1)}, bf16[320,512]{1,0:T(8,128)(2,1)S(1)}, u32[]{:S(2)}, u32[]{:S(2)}) collective-permute-start(bf16[320,512]{1,0:T(8,128)(2,1)S(1)} %get-tuple-element.79), channel_id=1, source_target_pairs={{0,2},{1,3},{2,0},{3,1},{4,6},{5,7},{6,4},{7,5},{8,10},{9,11},{10,... | collective-permute-start | bytes 983048 | tf_op jit(solution)/shard_map/ppermute | solution.py:584
  34.1 15.1 %collective-permute-start.13 = (bf16[320,512]{1,0:T(8,128)(2,1)S(1)}, bf16[320,512]{1,0:T(8,128)(2,1)S(1)}, u32[]{:S(2)}, u32[]{:S(2)}) collective-permute-start(bf16[320,512]{1,0:T(8,128)(2,1)S(1)} %get-tuple-element.80), channel_id=1, source_target_pairs={{0,2},{1,3},{2,0},{3,1},{4,6},{5,7},{6,4},{7,5},{8,10},{9,11},{10,... | collective-permute-start | bytes 983048 | tf_op jit(solution)/shard_map/ppermute | solution.py:584
  38.8 11.6 %collective-permute-start.11 = (bf16[640,256]{1,0:T(8,128)(2,1)S(1)}, bf16[640,256]{1,0:T(8,128)(2,1)S(1)}, u32[]{:S(2)}, u32[]{:S(2)}) collective-permute-start(bf16[640,256]{1,0:T(8,128)(2,1)S(1)} %shard_map.84.refs_1_.sent_ref), channel_id=1, source_target_pairs={{0,4},{4,0},{8,12},{12,8},{1,5},{5,1},{9,13},{13,9},{2,6},{6,2},{1... | collective-permute-start | bytes 983048 | tf_op jit(solution)/shard_map/ppermute | solution.py:532
  40.7 10.3 %collective-permute-start.10 = (bf16[640,256]{1,0:T(8,128)(2,1)S(1)}, bf16[640,256]{1,0:T(8,128)(2,1)S(1)}, u32[]{:S(2)}, u32[]{:S(2)}) collective-permute-start(bf16[640,256]{1,0:T(8,128)(2,1)S(1)} %get-tuple-element.75.prev_ref), channel_id=1, source_target_pairs={{4,8},{8,4},{0,1},{12,13},{5,9},{9,5},{1,0},{13,12},{6,10},{10,6},... | collective-permute-start | bytes 983048 | tf_op jit(solution)/shard_map/ppermute | solution.py:539
  47.2 8.5 %collective-permute-start.9 = (bf16[640,256]{1,0:T(8,128)(2,1)S(1)}, bf16[640,256]{1,0:T(8,128)(2,1)S(1)}, u32[]{:S(2)}, u32[]{:S(2)}) collective-permute-start(bf16[640,256]{1,0:T(8,128)(2,1)S(1)} %shard_map.87.refs_2_.sent_ref), channel_id=1, source_target_pairs={{0,4},{4,0},{8,12},{12,8},{1,5},{5,1},{9,13},{13,9},{2,6},{6,2},{1... | collective-permute-start | bytes 983048 | tf_op jit(solution)/shard_map/ppermute | solution.py:532
  49.4 9.1 %collective-permute-start.14 = (bf16[320,512]{1,0:T(8,128)(2,1)S(1)}, bf16[320,512]{1,0:T(8,128)(2,1)S(1)}, u32[]{:S(2)}, u32[]{:S(2)}) collective-permute-start(bf16[320,512]{1,0:T(8,128)(2,1)S(1)} %get-tuple-element.84.refs_0_), channel_id=1, source_target_pairs={{0,1},{1,0},{2,3},{3,2},{4,5},{5,4},{6,7},{7,6},{8,9},{9,8},{10,11... | collective-permute-start | bytes 983048 | tf_op jit(solution)/shard_map/ppermute | solution.py:594
  50.3 8.2 %collective-permute-start.15 = (bf16[320,512]{1,0:T(8,128)(2,1)S(1)}, bf16[320,512]{1,0:T(8,128)(2,1)S(1)}, u32[]{:S(2)}, u32[]{:S(2)}) collective-permute-start(bf16[320,512]{1,0:T(8,128)(2,1)S(1)} %get-tuple-element.85.refs_1_), channel_id=1, source_target_pairs={{0,1},{1,0},{2,3},{3,2},{4,5},{5,4},{6,7},{7,6},{8,9},{9,8},{10,11... | collective-permute-start | bytes 983048 | tf_op jit(solution)/shard_map/ppermute | solution.py:594
  50.5 12.0 %collective-permute-start.16 = (bf16[640,256]{1,0:T(8,128)(2,1)S(1)}, bf16[640,256]{1,0:T(8,128)(2,1)S(1)}, u32[]{:S(2)}, u32[]{:S(2)}) collective-permute-start(bf16[640,256]{1,0:T(8,128)(2,1)S(1)} %get-tuple-element.82.refs_1_), channel_id=1, source_target_pairs={{4,8},{8,4},{0,1},{12,13},{5,9},{9,5},{1,0},{13,12},{6,10},{10,6},... | collective-permute-start | bytes 983048 | tf_op jit(solution)/shard_map/ppermute | solution.py:539
  51.1 11.8 %collective-permute-start.19 = (bf16[640,256]{1,0:T(8,128)(2,1)S(1)}, bf16[640,256]{1,0:T(8,128)(2,1)S(1)}, u32[]{:S(2)}, u32[]{:S(2)}) collective-permute-start(bf16[640,256]{1,0:T(8,128)(2,1)S(1)} %shard_map.90.refs_1_.sent_ref), channel_id=1, source_target_pairs={{0,4},{4,0},{8,12},{12,8},{1,5},{5,1},{9,13},{13,9},{2,6},{6,2},{1... | collective-permute-start | bytes 983048 | tf_op jit(solution)/shard_map/ppermute | solution.py:532
  55.8 12.4 %collective-permute-start.18 = (bf16[640,256]{1,0:T(8,128)(2,1)S(1)}, bf16[640,256]{1,0:T(8,128)(2,1)S(1)}, u32[]{:S(2)}, u32[]{:S(2)}) collective-permute-start(bf16[640,256]{1,0:T(8,128)(2,1)S(1)} %get-tuple-element.83.prev_ref), channel_id=1, source_target_pairs={{4,8},{8,4},{0,1},{12,13},{5,9},{9,5},{1,0},{13,12},{6,10},{10,6},... | collective-permute-start | bytes 983048 | tf_op jit(solution)/shard_map/ppermute | solution.py:539
  62.6 9.4 %collective-permute-start.17 = (bf16[640,256]{1,0:T(8,128)(2,1)S(1)}, bf16[640,256]{1,0:T(8,128)(2,1)S(1)}, u32[]{:S(2)}, u32[]{:S(2)}) collective-permute-start(bf16[640,256]{1,0:T(8,128)(2,1)S(1)} %shard_map.94.refs_1_.sent_ref), channel_id=1, source_target_pairs={{0,4},{4,0},{8,12},{12,8},{1,5},{5,1},{9,13},{13,9},{2,6},{6,2},{1... | collective-permute-start | bytes 983048 | tf_op jit(solution)/shard_map/ppermute | solution.py:532
  63.1 13.8 %collective-permute-start.21 = (bf16[640,256]{1,0:T(8,128)(2,1)S(1)}, bf16[640,256]{1,0:T(8,128)(2,1)S(1)}, u32[]{:S(2)}, u32[]{:S(2)}) collective-permute-start(bf16[640,256]{1,0:T(8,128)(2,1)S(1)} %get-tuple-element.92.order_ref), channel_id=1, source_target_pairs={{4,8},{8,4},{0,1},{12,13},{5,9},{9,5},{1,0},{13,12},{6,10},{10,6},... | collective-permute-start | bytes 983048 | tf_op jit(solution)/shard_map/ppermute | solution.py:539
  68.3 12.3 %collective-permute-start.22 = (bf16[640,256]{1,0:T(8,128)(2,1)S(1)}, bf16[640,256]{1,0:T(8,128)(2,1)S(1)}, u32[]{:S(2)}, u32[]{:S(2)}) collective-permute-start(bf16[640,256]{1,0:T(8,128)(2,1)S(1)} %shard_map.97.refs_1_.sent_ref), channel_id=1, source_target_pairs={{0,4},{4,0},{8,12},{12,8},{1,5},{5,1},{9,13},{13,9},{2,6},{6,2},{1... | collective-permute-start | bytes 983048 | tf_op jit(solution)/shard_map/ppermute | solution.py:532
  72.1 8.5 %collective-permute-start.20 = (bf16[640,256]{1,0:T(8,128)(2,1)S(1)}, bf16[640,256]{1,0:T(8,128)(2,1)S(1)}, u32[]{:S(2)}, u32[]{:S(2)}) collective-permute-start(bf16[640,256]{1,0:T(8,128)(2,1)S(1)} %get-tuple-element.94.order_ref), channel_id=1, source_target_pairs={{4,8},{8,4},{0,1},{12,13},{5,9},{9,5},{1,0},{13,12},{6,10},{10,6},... | collective-permute-start | bytes 983048 | tf_op jit(solution)/shard_map/ppermute | solution.py:539
  77.0 13.1 %collective-permute-start.24 = (bf16[640,256]{1,0:T(8,128)(2,1)S(1)}, bf16[640,256]{1,0:T(8,128)(2,1)S(1)}, u32[]{:S(2)}, u32[]{:S(2)}) collective-permute-start(bf16[640,256]{1,0:T(8,128)(2,1)S(1)} %shard_map.100.order_ref.sent_ref), channel_id=1, source_target_pairs={{0,4},{4,0},{8,12},{12,8},{1,5},{5,1},{9,13},{13,9},{2,6},{6,2},{1... | collective-permute-start | bytes 983048 | tf_op jit(solution)/shard_map/ppermute | solution.py:532
  80.9 12.7 %collective-permute-start.23 = (bf16[640,256]{1,0:T(8,128)(2,1)S(1)}, bf16[640,256]{1,0:T(8,128)(2,1)S(1)}, u32[]{:S(2)}, u32[]{:S(2)}) collective-permute-start(bf16[640,256]{1,0:T(8,128)(2,1)S(1)} %shard_map.103.order_ref.sent_ref), channel_id=1, source_target_pairs={{0,4},{4,0},{8,12},{12,8},{1,5},{5,1},{9,13},{13,9},{2,6},{6,2},{1... | collective-permute-start | bytes 983048 | tf_op jit(solution)/shard_map/ppermute | solution.py:532
  97.3 3.6 %collective-permute-start.25 = (f32[8,128]{1,0:T(8,128)S(1)}, f32[8,128]{1,0:T(8,128)S(1)}, u32[]{:S(2)}, u32[]{:S(2)}) collective-permute-start(f32[8,128]{1,0:T(8,128)S(1)} %get-tuple-element.102), channel_id=1, source_target_pairs={{0,4},{4,0},{8,12},{12,8},{1,5},{5,1},{9,13},{13,9},{2,6},{6,2},{1... | collective-permute-start | bytes 12296 | tf_op jit(solution)/shard_map/ppermute | solution.py:614
  97.3 3.5 %collective-permute-start.26 = (f32[8,128]{1,0:T(8,128)S(1)}, f32[8,128]{1,0:T(8,128)S(1)}, u32[]{:S(2)}, u32[]{:S(2)}) collective-permute-start(f32[8,128]{1,0:T(8,128)S(1)} %get-tuple-element.103), channel_id=1, source_target_pairs={{0,8},{4,12},{8,0},{12,4},{1,9},{5,13},{9,1},{13,5},{2,10},{6,14},... | collective-permute-start | bytes 12296 | tf_op jit(solution)/shard_map/ppermute | solution.py:614
  98.7 4.3 %collective-permute-start.27 = (f32[8,128]{1,0:T(8,128)S(1)}, f32[8,128]{1,0:T(8,128)S(1)}, u32[]{:S(2)}, u32[]{:S(2)}) collective-permute-start(f32[8,128]{1,0:T(8,128)S(1)} %get-tuple-element.104), channel_id=1, source_target_pairs={{0,12},{4,8},{8,4},{12,0},{1,13},{5,9},{9,5},{13,1},{2,14},{6,10},... | collective-permute-start | bytes 12296 | tf_op jit(solution)/shard_map/ppermute | solution.py:614
  102.9 4.7 %collective-permute-start.28 = (f32[8,128]{1,0:T(8,128)S(1)}, f32[8,128]{1,0:T(8,128)S(1)}, u32[]{:S(2)}, u32[]{:S(2)}) collective-permute-start(f32[8,128]{1,0:T(8,128)S(1)} %shard_map.108.refs_0_), channel_id=1, source_target_pairs={{0,1},{1,0},{2,3},{3,2},{4,5},{5,4},{6,7},{7,6},{8,9},{9,8},{10,11... | collective-permute-start | bytes 12296 | tf_op jit(solution)/shard_map/ppermute | solution.py:619
  105.9 2.5 %collective-permute-start.29 = (f32[8,128]{1,0:T(8,128)S(1)}, f32[8,128]{1,0:T(8,128)S(1)}, u32[]{:S(2)}, u32[]{:S(2)}) collective-permute-start(f32[8,128]{1,0:T(8,128)S(1)} %shard_map.108.refs_0_), channel_id=1, source_target_pairs={{0,2},{1,3},{2,0},{3,1},{4,6},{5,7},{6,4},{7,5},{8,10},{9,11},{10,... | collective-permute-start | bytes 12296 | tf_op jit(solution)/shard_map/ppermute | solution.py:619
  107.1 3.0 %collective-permute-start.30 = (f32[8,128]{1,0:T(8,128)S(1)}, f32[8,128]{1,0:T(8,128)S(1)}, u32[]{:S(2)}, u32[]{:S(2)}) collective-permute-start(f32[8,128]{1,0:T(8,128)S(1)} %shard_map.108.refs_0_), channel_id=1, source_target_pairs={{0,3},{1,2},{2,1},{3,0},{4,7},{5,6},{6,5},{7,4},{8,11},{9,10},{10,... | collective-permute-start | bytes 12296 | tf_op jit(solution)/shard_map/ppermute | solution.py:619

commit v2 on v1

--- a/solution.py
+++ b/solution.py
@@ -556,7 +556,7 @@
             k == 0, norm_scale if k == count - 1 else None, halves,
         )
 
-    early = min(LAG + 2, count)
+    early = min(LAG + 1, count)
     widths = [width for _, width in chunks]
     parts, narrow = in_part(
         act_train, act_query, basis_in, act_query, chunks[:1], [widths[0]]

time: 111 us -> 111 us (level)
  transfers between devices with their start and end apart: 31 -> 31, of which waited for: 7 -> 7; matrix products, arithmetic and copies ran while one was open for 0% -> 0% of each run, Pallas kernels for 50% -> 51%
where the time goes in v2:
time: 111 us; the launch traced here: 110 us
  Pallas kernels  62.4 us (56%)
  starting transfers between devices  36.5 us (33%)
  waiting for transfers between devices  10.9 us (10%)
    pallas_call x8, Pallas kernels, score_part(): pl.pallas_call(functools.partial(score_kernel, start, scale, len(out_shap...  28.2 us
    pallas_call x2, Pallas kernels, out_part(): pl.pallas_call(functools.partial(out_kernel, begin, count, last), in_spec...  15.4 us
    ppermute x11, starting transfers between devices, swap(): got[j] = lax.ppermute(payload, 'row', outer)  15 us
    pallas_call x3, Pallas kernels, in_part(): pl.pallas_call(functools.partial(in_kernel, chunks, len(narrow), groups),...  11.8 us
    ppermute x8, starting transfers between devices, meet(): got_mid[j] = lax.ppermute(thin[0], ('row', 'col'), inner)  10.7 us
    ppermute x3, starting transfers between devices, on_device(): lax.ppermute(owned, 'col', [(d, d ^ step) for d in range(n_col)])  4.21 us
    ppermute x11, waiting for transfers between devices, swap(): got[j] = lax.ppermute(payload, 'row', outer)  3.88 us
    pallas_call x1, Pallas kernels, inverse_part(): pl.pallas_call(functools.partial(inverse_kernel, chunks), in_specs=[ANY_S...  3.86 us
  transfers between devices with their start and end apart: 31, of which 7 were waited for; matrix products, arithmetic and copies ran while one was open for 0% of the time, Pallas kernels for 51%

profile of v2, /device:TPU:1, one launch (start us, length us, event | category | flops | bytes accessed | tf_op | source)
XLA Modules:
  0.0 110.2 jit_solution(4397943141146055151)
XLA Ops:
  0.0 2.4 %shard_map.73 = (f32[640,256]{1,0:T(8,128)S(1)}, bf16[640,256]{1,0:T(8,128)(2,1)S(1)}) custom-call(bf16[512,2048]{1,0:T(8,128)(2,1)} %train_ref.9, bf16[128,2048]{1,0:T(8,128)(2,1)} %query_ref.9, bf16[2048,2048]{1,0:T(8,128)(2,1)} %basis_ref.9, bf16[128,2048]{1,0:T(8,128)(2,1)} %query_ref.9), custom_call_target="tpu_custom_call" | custom-call | flops 1024 | bytes 1024 | tf_op jit(solution)/shard_map/pallas_call | solution.py:123
  2.5 2.2 %collective-permute-start = (bf16[640,256]{1,0:T(8,128)(2,1)S(1)}, bf16[640,256]{1,0:T(8,128)(2,1)S(1)}, u32[]{:S(2)}, u32[]{:S(2)}) collective-permute-start(bf16[640,256]{1,0:T(8,128)(2,1)S(1)} %get-tuple-element.56), channel_id=1, source_target_pairs={{0,4},{4,0},{8,12},{12,8},{1,5},{5,1},{9,13},{13,9},{2,6},{6,2},{1... | collective-permute-start | bytes 983048 | tf_op jit(solution)/shard_map/ppermute | solution.py:532
  4.6 4.3 %shard_map.74 = (f32[640,256]{1,0:T(8,128)S(1)}, f32[640,256]{1,0:T(8,128)S(1)}, f32[640,256]{1,0:T(8,128)S(1)}, bf16[640,256]{1,0:T(8,128)(2,1)S(1)}) custom-call(bf16[512,2048]{1,0:T(8,128)(2,1)} %train_ref.9, bf16[128,2048]{1,0:T(8,128)(2,1)} %query_ref.9, bf16[2048,2048]{1,0:T(8,128)(2,1)} %basis_ref.9, f32[640,256]{1,0:T(8,128)S(1)} %get-tuple-element.55.prev_ref.keep_ref), custom_call_target="tpu_custom_call" | custom-call | flops 1024 | bytes 1024 | tf_op jit(solution)/shard_map/pallas_call | solution.py:123
  9.0 5.0 %shard_map.75.refs_2_.refs_0_ = f32[640,1024]{1,0:T(8,128)S(1)} custom-call(bf16[512,7168]{1,0:T(8,128)(2,1)} %train_ref.8, bf16[128,7168]{1,0:T(8,128)(2,1)} %query_ref.8, bf16[7168,1024]{1,0:T(8,128)(2,1)} %basis_ref.8, f32[640,256]{1,0:T(8,128)S(1)} %get-tuple-element.58.prev_ref.refs_0_.keep_ref), custom_call_target="tpu_custom_call" | custom-call | flops 1024 | bytes 1024 | tf_op jit(solution)/shard_map/pallas_call | solution.py:211
  14.2 1.5 %collective-permute-start.3 = (bf16[640,256]{1,0:T(8,128)(2,1)S(1)}, bf16[640,256]{1,0:T(8,128)(2,1)S(1)}, u32[]{:S(2)}, u32[]{:S(2)}) collective-permute-start(bf16[640,256]{1,0:T(8,128)(2,1)S(1)} %get-tuple-element.63), channel_id=1, source_target_pairs={{0,4},{4,0},{8,12},{12,8},{1,5},{5,1},{9,13},{13,9},{2,6},{6,2},{1... | collective-permute-start | bytes 983048 | tf_op jit(solution)/shard_map/ppermute | solution.py:532
  15.7 1.5 %collective-permute-start.4 = (bf16[640,256]{1,0:T(8,128)(2,1)S(1)}, bf16[640,256]{1,0:T(8,128)(2,1)S(1)}, u32[]{:S(2)}, u32[]{:S(2)}) collective-permute-start(bf16[640,256]{1,0:T(8,128)(2,1)S(1)} %get-tuple-element.59.prev_ref), channel_id=1, source_target_pairs={{4,8},{8,4},{0,1},{12,13},{5,9},{9,5},{1,0},{13,12},{6,10},{10,6},... | collective-permute-start | bytes 983048 | tf_op jit(solution)/shard_map/ppermute | solution.py:539
  17.2 10.3 %shard_map.77 = (f32[320,1024]{1,0:T(8,128)S(1)}, f32[320,512]{1,0:T(8,128)S(1)}, f32[320,512]{1,0:T(8,128)S(1)}) custom-call(bf16[512,7168]{1,0:T(8,128)(2,1)} %train_ref.8, bf16[128,7168]{1,0:T(8,128)(2,1)} %query_ref.8, bf16[7168,1024]{1,0:T(8,128)(2,1)} %basis_ref.8, bf16[640,256]{1,0:T(8,128)(2,1)S(1)} %get-tuple-element.59.prev_ref, ...), custom_call_target="tpu_custom_call" | custom-call | flops 6710886400 | bytes 1024 | tf_op jit(solution)/shard_map/pallas_call | solution.py:211
  28.5 2.5 %collective-permute-start.7 = (bf16[640,256]{1,0:T(8,128)(2,1)S(1)}, bf16[640,256]{1,0:T(8,128)(2,1)S(1)}, u32[]{:S(2)}, u32[]{:S(2)}) collective-permute-start(bf16[640,256]{1,0:T(8,128)(2,1)S(1)} %shard_map.80.refs_1_.sent_ref), channel_id=1, source_target_pairs={{0,4},{4,0},{8,12},{12,8},{1,5},{5,1},{9,13},{13,9},{2,6},{6,2},{1... | collective-permute-start | bytes 983048 | tf_op jit(solution)/shard_map/ppermute | solution.py:532
  33.5 5.1 %shard_map.83 = (f32[640,256]{1,0:T(8,128)S(1)}, f32[640,256]{1,0:T(8,128)S(1)}, f32[640,256]{1,0:T(8,128)S(1)}, f32[640,256]{1,0:T(8,128)S(1)}) custom-call(bf16[512,2048]{1,0:T(8,128)(2,1)} %train_ref.9, bf16[128,2048]{1,0:T(8,128)(2,1)} %query_ref.9, bf16[2048,2048]{1,0:T(8,128)(2,1)} %basis_ref.9, f32[320,1024]{1,0:T(8,128)S(1)} %get-tuple-element.69.prev_ref.keep_ref), custom_call_target="tpu_custom_call" | custom-call | flops 1024 | bytes 1024 | tf_op jit(solution)/shard_map/pallas_call | solution.py:123
  38.8 1.4 %collective-permute-start.11 = (bf16[640,256]{1,0:T(8,128)(2,1)S(1)}, bf16[640,256]{1,0:T(8,128)(2,1)S(1)}, u32[]{:S(2)}, u32[]{:S(2)}) collective-permute-start(bf16[640,256]{1,0:T(8,128)(2,1)S(1)} %shard_map.84.refs_1_.sent_ref), channel_id=1, source_target_pairs={{0,4},{4,0},{8,12},{12,8},{1,5},{5,1},{9,13},{13,9},{2,6},{6,2},{1... | collective-permute-start | bytes 983048 | tf_op jit(solution)/shard_map/ppermute | solution.py:532
  40.2 2.1 %collective-permute-start.10 = (bf16[640,256]{1,0:T(8,128)(2,1)S(1)}, bf16[640,256]{1,0:T(8,128)(2,1)S(1)}, u32[]{:S(2)}, u32[]{:S(2)}) collective-permute-start(bf16[640,256]{1,0:T(8,128)(2,1)S(1)} %get-tuple-element.75.prev_ref), channel_id=1, source_target_pairs={{4,8},{8,4},{0,1},{12,13},{5,9},{9,5},{1,0},{13,12},{6,10},{10,6},... | collective-permute-start | bytes 983048 | tf_op jit(solution)/shard_map/ppermute | solution.py:539
  42.3 3.9 %shard_map.86 = (f32[1024,256]{1,0:T(8,128)S(1)}, f32[1024,256]{1,0:T(8,128)S(1)}, f32[1024,256]{1,0:T(8,128)S(1)}, f32[1024,256]{1,0:T(8,128)S(1)}, f32[1024,25...) custom-call(f32[1024,2048]{1,0:T(8,128)} %corr_ref.1, ...), custom_call_target="tpu_custom_call" | custom-call | flops 1024 | bytes 1024 | tf_op jit(solution)/shard_map/pallas_call | solution.py:332
  46.8 1.6 %collective-permute-done.13.refs_1_ = bf16[320,512]{1,0:T(8,128)(2,1)S(1)} collective-permute-done((bf16[320,512]{1,0:T(8,128)(2,1)S(1)}, bf16[320,512]{1,0:T(8,128)(2,1)S(1)}, u32[]{:S(2)}, u32[]{:S(2)}) %collective-permute-start.13) | collective-permute-done | bytes 327712 | tf_op jit(solution)/shard_map/ppermute | solution.py:584
  50.2 3.6 %collective-permute-start.19 = (bf16[640,256]{1,0:T(8,128)(2,1)S(1)}, bf16[640,256]{1,0:T(8,128)(2,1)S(1)}, u32[]{:S(2)}, u32[]{:S(2)}) collective-permute-start(bf16[640,256]{1,0:T(8,128)(2,1)S(1)} %shard_map.90.refs_1_.sent_ref), channel_id=1, source_target_pairs={{0,4},{4,0},{8,12},{12,8},{1,5},{5,1},{9,13},{13,9},{2,6},{6,2},{1... | collective-permute-start | bytes 983048 | tf_op jit(solution)/shard_map/ppermute | solution.py:532
  55.0 2.7 %collective-permute-start.18 = (bf16[640,256]{1,0:T(8,128)(2,1)S(1)}, bf16[640,256]{1,0:T(8,128)(2,1)S(1)}, u32[]{:S(2)}, u32[]{:S(2)}) collective-permute-start(bf16[640,256]{1,0:T(8,128)(2,1)S(1)} %get-tuple-element.83.prev_ref), channel_id=1, source_target_pairs={{4,8},{8,4},{0,1},{12,13},{5,9},{9,5},{1,0},{13,12},{6,10},{10,6},... | collective-permute-start | bytes 983048 | tf_op jit(solution)/shard_map/ppermute | solution.py:539
  58.1 3.5 %shard_map.93.refs_1_.prev_ref = f32[512,128]{1,0:T(8,128)S(1)} custom-call(bf16[512,1024]{1,0:T(8,128)(2,1)S(1)} %get-tuple-element.86.gt_ref.prev_ref.order_ref, bf16[1024,128]{1,0:T(8,128)(2,1)S(1)} %get-tuple-element.87.gq_ref, f32[1024,256]{1,0:T(8,128)S(1)} %get-tuple-element.76.refs_1_.inv_ref, bf16[640,256]{1,0:T(8,128)(2,1)S(1)} %shard_map.80.refs_1_.sent_ref, ...), custom_call_target="tpu_custom_call" | custom-call | flops 1024 | bytes 1024 | tf_op jit(solution)/shard_map/pallas_call | solution.py:445
  62.3 1.6 %collective-permute-start.21 = (bf16[640,256]{1,0:T(8,128)(2,1)S(1)}, bf16[640,256]{1,0:T(8,128)(2,1)S(1)}, u32[]{:S(2)}, u32[]{:S(2)}) collective-permute-start(bf16[640,256]{1,0:T(8,128)(2,1)S(1)} %get-tuple-element.92.order_ref), channel_id=1, source_target_pairs={{4,8},{8,4},{0,1},{12,13},{5,9},{9,5},{1,0},{13,12},{6,10},{10,6},... | collective-permute-start | bytes 983048 | tf_op jit(solution)/shard_map/ppermute | solution.py:539
  63.9 3.5 %shard_map.96.refs_0_.prev_ref = f32[512,128]{1,0:T(8,128)S(1)} custom-call(bf16[512,1024]{1,0:T(8,128)(2,1)S(1)} %get-tuple-element.86.gt_ref.prev_ref.order_ref, bf16[1024,128]{1,0:T(8,128)(2,1)S(1)} %get-tuple-element.87.gq_ref, f32[1024,256]{1,0:T(8,128)S(1)} %get-tuple-element.91.inv_ref, bf16[640,256]{1,0:T(8,128)(2,1)S(1)} %shard_map.84.refs_1_.sent_ref, ...), custom_call_target="tpu_custom_call" | custom-call | flops 1024 | bytes 1024 | tf_op jit(solution)/shard_map/pallas_call | solution.py:445
  68.5 2.6 %collective-permute-done.17.refs_0_.got_ref = bf16[640,256]{1,0:T(8,128)(2,1)S(1)} collective-permute-done((bf16[640,256]{1,0:T(8,128)(2,1)S(1)}, bf16[640,256]{1,0:T(8,128)(2,1)S(1)}, u32[]{:S(2)}, u32[]{:S(2)}) %collective-permute-start.17) | collective-permute-done | bytes 327712 | tf_op jit(solution)/shard_map/ppermute | solution.py:532
  71.2 1.3 %collective-permute-start.20 = (bf16[640,256]{1,0:T(8,128)(2,1)S(1)}, bf16[640,256]{1,0:T(8,128)(2,1)S(1)}, u32[]{:S(2)}, u32[]{:S(2)}) collective-permute-start(bf16[640,256]{1,0:T(8,128)(2,1)S(1)} %get-tuple-element.94.order_ref), channel_id=1, source_target_pairs={{4,8},{8,4},{0,1},{12,13},{5,9},{9,5},{1,0},{13,12},{6,10},{10,6},... | collective-permute-start | bytes 983048 | tf_op jit(solution)/shard_map/ppermute | solution.py:539
  72.5 3.5 %shard_map.99.refs_0_.prev_ref = f32[512,128]{1,0:T(8,128)S(1)} custom-call(bf16[512,1024]{1,0:T(8,128)(2,1)S(1)} %get-tuple-element.86.gt_ref.prev_ref.order_ref, bf16[1024,128]{1,0:T(8,128)(2,1)S(1)} %get-tuple-element.87.gq_ref, f32[1024,256]{1,0:T(8,128)S(1)} %get-tuple-element.96.inv_ref, bf16[640,256]{1,0:T(8,128)(2,1)S(1)} %shard_map.87.refs_2_.sent_ref, ...), custom_call_target="tpu_custom_call" | custom-call | flops 1024 | bytes 1024 | tf_op jit(solution)/shard_map/pallas_call | solution.py:445
  76.2 3.5 %shard_map.101.first_ref.prev_ref = f32[512,128]{1,0:T(8,128)S(1)} custom-call(bf16[512,1024]{1,0:T(8,128)(2,1)S(1)} %get-tuple-element.86.gt_ref.prev_ref.order_ref, bf16[1024,128]{1,0:T(8,128)(2,1)S(1)} %get-tuple-element.87.gq_ref, f32[1024,256]{1,0:T(8,128)S(1)} %get-tuple-element.95.inv_ref, bf16[640,256]{1,0:T(8,128)(2,1)S(1)} %shard_map.90.refs_1_.sent_ref, ...), custom_call_target="tpu_custom_call" | custom-call | flops 1024 | bytes 1024 | tf_op jit(solution)/shard_map/pallas_call | solution.py:445
  80.1 2.2 %collective-permute-start.23 = (bf16[640,256]{1,0:T(8,128)(2,1)S(1)}, bf16[640,256]{1,0:T(8,128)(2,1)S(1)}, u32[]{:S(2)}, u32[]{:S(2)}) collective-permute-start(bf16[640,256]{1,0:T(8,128)(2,1)S(1)} %shard_map.103.order_ref.sent_ref), channel_id=1, source_target_pairs={{0,4},{4,0},{8,12},{12,8},{1,5},{5,1},{9,13},{13,9},{2,6},{6,2},{1... | collective-permute-start | bytes 983048 | tf_op jit(solution)/shard_map/ppermute | solution.py:532
  82.2 3.5 %shard_map.104.prev_ref = f32[512,128]{1,0:T(8,128)S(1)} custom-call(bf16[512,1024]{1,0:T(8,128)(2,1)S(1)} %get-tuple-element.86.gt_ref.prev_ref.order_ref, bf16[1024,128]{1,0:T(8,128)(2,1)S(1)} %get-tuple-element.87.gq_ref, f32[1024,256]{1,0:T(8,128)S(1)} %get-tuple-element.100.inv_ref, bf16[640,256]{1,0:T(8,128)(2,1)S(1)} %shard_map.94.refs_1_.sent_ref, ...), custom_call_target="tpu_custom_call" | custom-call | flops 1024 | bytes 1024 | tf_op jit(solution)/shard_map/pallas_call | solution.py:445
  85.8 3.5 %shard_map.105.prev_ref = f32[512,128]{1,0:T(8,128)S(1)} custom-call(bf16[512,1024]{1,0:T(8,128)(2,1)S(1)} %get-tuple-element.86.gt_ref.prev_ref.order_ref, bf16[1024,128]{1,0:T(8,128)(2,1)S(1)} %get-tuple-element.87.gq_ref, f32[1024,256]{1,0:T(8,128)S(1)} %get-tuple-element.99.inv_ref, bf16[640,256]{1,0:T(8,128)(2,1)S(1)} %shard_map.97.refs_1_.sent_ref, ...), custom_call_target="tpu_custom_call" | custom-call | flops 1024 | bytes 1024 | tf_op jit(solution)/shard_map/pallas_call | solution.py:445
  89.3 3.5 %shard_map.106.prev_ref = f32[512,128]{1,0:T(8,128)S(1)} custom-call(bf16[512,1024]{1,0:T(8,128)(2,1)S(1)} %get-tuple-element.86.gt_ref.prev_ref.order_ref, bf16[1024,128]{1,0:T(8,128)(2,1)S(1)} %get-tuple-element.87.gq_ref, f32[1024,256]{1,0:T(8,128)S(1)} %get-tuple-element.98.inv_ref, bf16[640,256]{1,0:T(8,128)(2,1)S(1)} %shard_map.100.order_ref.sent_ref, ...), custom_call_target="tpu_custom_call" | custom-call | flops 1024 | bytes 1024 | tf_op jit(solution)/shard_map/pallas_call | solution.py:445
  92.8 3.6 %shard_map.107 = (f32[8,128]{1,0:T(8,128)S(1)}, f32[8,128]{1,0:T(8,128)S(1)}, f32[8,128]{1,0:T(8,128)S(1)}, f32[8,128]{1,0:T(8,128)S(1)}) custom-call(bf16[512,1024]{1,0:T(8,128)(2,1)S(1)} %get-tuple-element.86.gt_ref.prev_ref.order_ref, bf16[1024,128]{1,0:T(8,128)(2,1)S(1)} %get-tuple-element.87.gq_ref, f32[1024,256]{1,0:T(8,128)S(1)} %get-tuple-element.88.inv_ref, ...), custom_call_target="tpu_custom_call" | custom-call | flops 1024 | bytes 1024 | tf_op jit(solution)/shard_map/pallas_call | solution.py:445
  96.5 2.1 %collective-permute-start.26 = (f32[8,128]{1,0:T(8,128)S(1)}, f32[8,128]{1,0:T(8,128)S(1)}, u32[]{:S(2)}, u32[]{:S(2)}) collective-permute-start(f32[8,128]{1,0:T(8,128)S(1)} %get-tuple-element.103), channel_id=1, source_target_pairs={{0,8},{4,12},{8,0},{12,4},{1,9},{5,13},{9,1},{13,5},{2,10},{6,14},... | collective-permute-start | bytes 12296 | tf_op jit(solution)/shard_map/ppermute | solution.py:614
  98.6 1.4 %collective-permute-start.27 = (f32[8,128]{1,0:T(8,128)S(1)}, f32[8,128]{1,0:T(8,128)S(1)}, u32[]{:S(2)}, u32[]{:S(2)}) collective-permute-start(f32[8,128]{1,0:T(8,128)S(1)} %get-tuple-element.104), channel_id=1, source_target_pairs={{0,12},{4,8},{8,4},{12,0},{1,13},{5,9},{9,5},{13,1},{2,14},{6,10},... | collective-permute-start | bytes 12296 | tf_op jit(solution)/shard_map/ppermute | solution.py:614
  100.0 2.8 %collective-permute-done.27.refs_3_ = f32[8,128]{1,0:T(8,128)S(1)} collective-permute-done((f32[8,128]{1,0:T(8,128)S(1)}, f32[8,128]{1,0:T(8,128)S(1)}, u32[]{:S(2)}, u32[]{:S(2)}) %collective-permute-start.27) | collective-permute-done | bytes 4128 | tf_op jit(solution)/shard_map/ppermute | solution.py:614
  102.9 2.5 %collective-permute-start.28 = (f32[8,128]{1,0:T(8,128)S(1)}, f32[8,128]{1,0:T(8,128)S(1)}, u32[]{:S(2)}, u32[]{:S(2)}) collective-permute-start(f32[8,128]{1,0:T(8,128)S(1)} %shard_map.108.refs_0_), channel_id=1, source_target_pairs={{0,1},{1,0},{2,3},{3,2},{4,5},{5,4},{6,7},{7,6},{8,9},{9,8},{10,11... | collective-permute-start | bytes 12296 | tf_op jit(solution)/shard_map/ppermute | solution.py:619
  107.8 1.8 %collective-permute-done.30.refs_3_ = f32[8,128]{1,0:T(8,128)S(1)} collective-permute-done((f32[8,128]{1,0:T(8,128)S(1)}, f32[8,128]{1,0:T(8,128)S(1)}, u32[]{:S(2)}, u32[]{:S(2)}) %collective-permute-start.30) | collective-permute-done | bytes 4128 | tf_op jit(solution)/shard_map/ppermute | solution.py:619
  (67 shorter events, 13.2 us)
Async XLA Ops:
  2.5 11.6 %collective-permute-start = (bf16[640,256]{1,0:T(8,128)(2,1)S(1)}, bf16[640,256]{1,0:T(8,128)(2,1)S(1)}, u32[]{:S(2)}, u32[]{:S(2)}) collective-permute-start(bf16[640,256]{1,0:T(8,128)(2,1)S(1)} %get-tuple-element.56), channel_id=1, source_target_pairs={{0,4},{4,0},{8,12},{12,8},{1,5},{5,1},{9,13},{13,9},{2,6},{6,2},{1... | collective-permute-start | bytes 983048 | tf_op jit(solution)/shard_map/ppermute | solution.py:532
  8.9 19.2 %collective-permute-start.5 = (bf16[640,256]{1,0:T(8,128)(2,1)S(1)}, bf16[640,256]{1,0:T(8,128)(2,1)S(1)}, u32[]{:S(2)}, u32[]{:S(2)}) collective-permute-start(bf16[640,256]{1,0:T(8,128)(2,1)S(1)} %get-tuple-element.66), channel_id=1, source_target_pairs={{0,4},{4,0},{8,12},{12,8},{1,5},{5,1},{9,13},{13,9},{2,6},{6,2},{1... | collective-permute-start | bytes 983048 | tf_op jit(solution)/shard_map/ppermute | solution.py:532
  14.2 14.2 %collective-permute-start.3 = (bf16[640,256]{1,0:T(8,128)(2,1)S(1)}, bf16[640,256]{1,0:T(8,128)(2,1)S(1)}, u32[]{:S(2)}, u32[]{:S(2)}) collective-permute-start(bf16[640,256]{1,0:T(8,128)(2,1)S(1)} %get-tuple-element.63), channel_id=1, source_target_pairs={{0,4},{4,0},{8,12},{12,8},{1,5},{5,1},{9,13},{13,9},{2,6},{6,2},{1... | collective-permute-start | bytes 983048 | tf_op jit(solution)/shard_map/ppermute | solution.py:532
  15.7 12.7 %collective-permute-start.4 = (bf16[640,256]{1,0:T(8,128)(2,1)S(1)}, bf16[640,256]{1,0:T(8,128)(2,1)S(1)}, u32[]{:S(2)}, u32[]{:S(2)}) collective-permute-start(bf16[640,256]{1,0:T(8,128)(2,1)S(1)} %get-tuple-element.59.prev_ref), channel_id=1, source_target_pairs={{4,8},{8,4},{0,1},{12,13},{5,9},{9,5},{1,0},{13,12},{6,10},{10,6},... | collective-permute-start | bytes 983048 | tf_op jit(solution)/shard_map/ppermute | solution.py:539
  27.6 4.3 %collective-permute-start.1 = (f32[320,512]{1,0:T(8,128)S(1)}, f32[320,512]{1,0:T(8,128)S(1)}, u32[]{:S(2)}, u32[]{:S(2)}) collective-permute-start(f32[320,512]{1,0:T(8,128)S(1)} %get-tuple-element.61), channel_id=1, source_target_pairs={{0,1},{1,0},{2,3},{3,2},{4,5},{5,4},{6,7},{7,6},{8,9},{9,8},{10,11... | collective-permute-start | bytes 1966088 | tf_op jit(solution)/shard_map/ppermute | solution.py:575
  27.6 4.2 %collective-permute-start.2 = (f32[320,512]{1,0:T(8,128)S(1)}, f32[320,512]{1,0:T(8,128)S(1)}, u32[]{:S(2)}, u32[]{:S(2)}) collective-permute-start(f32[320,512]{1,0:T(8,128)S(1)} %get-tuple-element.62), channel_id=1, source_target_pairs={{0,1},{1,0},{2,3},{3,2},{4,5},{5,4},{6,7},{7,6},{8,9},{9,8},{10,11... | collective-permute-start | bytes 1966088 | tf_op jit(solution)/shard_map/ppermute | solution.py:575
  28.2 10.4 %collective-permute-start.8 = (bf16[640,256]{1,0:T(8,128)(2,1)S(1)}, bf16[640,256]{1,0:T(8,128)(2,1)S(1)}, u32[]{:S(2)}, u32[]{:S(2)}) collective-permute-start(bf16[640,256]{1,0:T(8,128)(2,1)S(1)} %get-tuple-element.67.first_ref), channel_id=1, source_target_pairs={{4,8},{8,4},{0,1},{12,13},{5,9},{9,5},{1,0},{13,12},{6,10},{10,6},... | collective-permute-start | bytes 983048 | tf_op jit(solution)/shard_map/ppermute | solution.py:539
  28.5 11.7 %collective-permute-start.7 = (bf16[640,256]{1,0:T(8,128)(2,1)S(1)}, bf16[640,256]{1,0:T(8,128)(2,1)S(1)}, u32[]{:S(2)}, u32[]{:S(2)}) collective-permute-start(bf16[640,256]{1,0:T(8,128)(2,1)S(1)} %shard_map.80.refs_1_.sent_ref), channel_id=1, source_target_pairs={{0,4},{4,0},{8,12},{12,8},{1,5},{5,1},{9,13},{13,9},{2,6},{6,2},{1... | collective-permute-start | bytes 983048 | tf_op jit(solution)/shard_map/ppermute | solution.py:532
  31.0 15.2 %collective-permute-start.6 = (bf16[640,256]{1,0:T(8,128)(2,1)S(1)}, bf16[640,256]{1,0:T(8,128)(2,1)S(1)}, u32[]{:S(2)}, u32[]{:S(2)}) collective-permute-start(bf16[640,256]{1,0:T(8,128)(2,1)S(1)} %get-tuple-element.68.refs_2_), channel_id=1, source_target_pairs={{4,8},{8,4},{0,1},{12,13},{5,9},{9,5},{1,0},{13,12},{6,10},{10,6},... | collective-permute-start | bytes 983048 | tf_op jit(solution)/shard_map/ppermute | solution.py:539
  32.0 14.8 %collective-permute-start.12 = (bf16[320,512]{1,0:T(8,128)(2,1)S(1)}, bf16[320,512]{1,0:T(8,128)(2,1)S(1)}, u32[]{:S(2)}, u32[]{:S(2)}) collective-permute-start(bf16[320,512]{1,0:T(8,128)(2,1)S(1)} %get-tuple-element.79), channel_id=1, source_target_pairs={{0,2},{1,3},{2,0},{3,1},{4,6},{5,7},{6,4},{7,5},{8,10},{9,11},{10,... | collective-permute-start | bytes 983048 | tf_op jit(solution)/shard_map/ppermute | solution.py:584
  33.3 15.1 %collective-permute-start.13 = (bf16[320,512]{1,0:T(8,128)(2,1)S(1)}, bf16[320,512]{1,0:T(8,128)(2,1)S(1)}, u32[]{:S(2)}, u32[]{:S(2)}) collective-permute-start(bf16[320,512]{1,0:T(8,128)(2,1)S(1)} %get-tuple-element.80), channel_id=1, source_target_pairs={{0,2},{1,3},{2,0},{3,1},{4,6},{5,7},{6,4},{7,5},{8,10},{9,11},{10,... | collective-permute-start | bytes 983048 | tf_op jit(solution)/shard_map/ppermute | solution.py:584
  38.8 10.8 %collective-permute-start.11 = (bf16[640,256]{1,0:T(8,128)(2,1)S(1)}, bf16[640,256]{1,0:T(8,128)(2,1)S(1)}, u32[]{:S(2)}, u32[]{:S(2)}) collective-permute-start(bf16[640,256]{1,0:T(8,128)(2,1)S(1)} %shard_map.84.refs_1_.sent_ref), channel_id=1, source_target_pairs={{0,4},{4,0},{8,12},{12,8},{1,5},{5,1},{9,13},{13,9},{2,6},{6,2},{1... | collective-permute-start | bytes 983048 | tf_op jit(solution)/shard_map/ppermute | solution.py:532
  40.2 9.9 %collective-permute-start.10 = (bf16[640,256]{1,0:T(8,128)(2,1)S(1)}, bf16[640,256]{1,0:T(8,128)(2,1)S(1)}, u32[]{:S(2)}, u32[]{:S(2)}) collective-permute-start(bf16[640,256]{1,0:T(8,128)(2,1)S(1)} %get-tuple-element.75.prev_ref), channel_id=1, source_target_pairs={{4,8},{8,4},{0,1},{12,13},{5,9},{9,5},{1,0},{13,12},{6,10},{10,6},... | collective-permute-start | bytes 983048 | tf_op jit(solution)/shard_map/ppermute | solution.py:539
  46.3 8.5 %collective-permute-start.9 = (bf16[640,256]{1,0:T(8,128)(2,1)S(1)}, bf16[640,256]{1,0:T(8,128)(2,1)S(1)}, u32[]{:S(2)}, u32[]{:S(2)}) collective-permute-start(bf16[640,256]{1,0:T(8,128)(2,1)S(1)} %shard_map.87.refs_2_.sent_ref), channel_id=1, source_target_pairs={{0,4},{4,0},{8,12},{12,8},{1,5},{5,1},{9,13},{13,9},{2,6},{6,2},{1... | collective-permute-start | bytes 983048 | tf_op jit(solution)/shard_map/ppermute | solution.py:532
  48.6 9.1 %collective-permute-start.14 = (bf16[320,512]{1,0:T(8,128)(2,1)S(1)}, bf16[320,512]{1,0:T(8,128)(2,1)S(1)}, u32[]{:S(2)}, u32[]{:S(2)}) collective-permute-start(bf16[320,512]{1,0:T(8,128)(2,1)S(1)} %get-tuple-element.84.refs_0_), channel_id=1, source_target_pairs={{0,1},{1,0},{2,3},{3,2},{4,5},{5,4},{6,7},{7,6},{8,9},{9,8},{10,11... | collective-permute-start | bytes 983048 | tf_op jit(solution)/shard_map/ppermute | solution.py:594
  49.5 8.2 %collective-permute-start.15 = (bf16[320,512]{1,0:T(8,128)(2,1)S(1)}, bf16[320,512]{1,0:T(8,128)(2,1)S(1)}, u32[]{:S(2)}, u32[]{:S(2)}) collective-permute-start(bf16[320,512]{1,0:T(8,128)(2,1)S(1)} %get-tuple-element.85.refs_1_), channel_id=1, source_target_pairs={{0,1},{1,0},{2,3},{3,2},{4,5},{5,4},{6,7},{7,6},{8,9},{9,8},{10,11... | collective-permute-start | bytes 983048 | tf_op jit(solution)/shard_map/ppermute | solution.py:594
  49.6 12.0 %collective-permute-start.16 = (bf16[640,256]{1,0:T(8,128)(2,1)S(1)}, bf16[640,256]{1,0:T(8,128)(2,1)S(1)}, u32[]{:S(2)}, u32[]{:S(2)}) collective-permute-start(bf16[640,256]{1,0:T(8,128)(2,1)S(1)} %get-tuple-element.82.refs_1_), channel_id=1, source_target_pairs={{4,8},{8,4},{0,1},{12,13},{5,9},{9,5},{1,0},{13,12},{6,10},{10,6},... | collective-permute-start | bytes 983048 | tf_op jit(solution)/shard_map/ppermute | solution.py:539
  50.2 11.8 %collective-permute-start.19 = (bf16[640,256]{1,0:T(8,128)(2,1)S(1)}, bf16[640,256]{1,0:T(8,128)(2,1)S(1)}, u32[]{:S(2)}, u32[]{:S(2)}) collective-permute-start(bf16[640,256]{1,0:T(8,128)(2,1)S(1)} %shard_map.90.refs_1_.sent_ref), channel_id=1, source_target_pairs={{0,4},{4,0},{8,12},{12,8},{1,5},{5,1},{9,13},{13,9},{2,6},{6,2},{1... | collective-permute-start | bytes 983048 | tf_op jit(solution)/shard_map/ppermute | solution.py:532
  55.0 12.4 %collective-permute-start.18 = (bf16[640,256]{1,0:T(8,128)(2,1)S(1)}, bf16[640,256]{1,0:T(8,128)(2,1)S(1)}, u32[]{:S(2)}, u32[]{:S(2)}) collective-permute-start(bf16[640,256]{1,0:T(8,128)(2,1)S(1)} %get-tuple-element.83.prev_ref), channel_id=1, source_target_pairs={{4,8},{8,4},{0,1},{12,13},{5,9},{9,5},{1,0},{13,12},{6,10},{10,6},... | collective-permute-start | bytes 983048 | tf_op jit(solution)/shard_map/ppermute | solution.py:539
  61.8 9.4 %collective-permute-start.17 = (bf16[640,256]{1,0:T(8,128)(2,1)S(1)}, bf16[640,256]{1,0:T(8,128)(2,1)S(1)}, u32[]{:S(2)}, u32[]{:S(2)}) collective-permute-start(bf16[640,256]{1,0:T(8,128)(2,1)S(1)} %shard_map.94.refs_1_.sent_ref), channel_id=1, source_target_pairs={{0,4},{4,0},{8,12},{12,8},{1,5},{5,1},{9,13},{13,9},{2,6},{6,2},{1... | collective-permute-start | bytes 983048 | tf_op jit(solution)/shard_map/ppermute | solution.py:532
  62.3 13.8 %collective-permute-start.21 = (bf16[640,256]{1,0:T(8,128)(2,1)S(1)}, bf16[640,256]{1,0:T(8,128)(2,1)S(1)}, u32[]{:S(2)}, u32[]{:S(2)}) collective-permute-start(bf16[640,256]{1,0:T(8,128)(2,1)S(1)} %get-tuple-element.92.order_ref), channel_id=1, source_target_pairs={{4,8},{8,4},{0,1},{12,13},{5,9},{9,5},{1,0},{13,12},{6,10},{10,6},... | collective-permute-start | bytes 983048 | tf_op jit(solution)/shard_map/ppermute | solution.py:539
  67.5 12.3 %collective-permute-start.22 = (bf16[640,256]{1,0:T(8,128)(2,1)S(1)}, bf16[640,256]{1,0:T(8,128)(2,1)S(1)}, u32[]{:S(2)}, u32[]{:S(2)}) collective-permute-start(bf16[640,256]{1,0:T(8,128)(2,1)S(1)} %shard_map.97.refs_1_.sent_ref), channel_id=1, source_target_pairs={{0,4},{4,0},{8,12},{12,8},{1,5},{5,1},{9,13},{13,9},{2,6},{6,2},{1... | collective-permute-start | bytes 983048 | tf_op jit(solution)/shard_map/ppermute | solution.py:532
  71.2 8.5 %collective-permute-start.20 = (bf16[640,256]{1,0:T(8,128)(2,1)S(1)}, bf16[640,256]{1,0:T(8,128)(2,1)S(1)}, u32[]{:S(2)}, u32[]{:S(2)}) collective-permute-start(bf16[640,256]{1,0:T(8,128)(2,1)S(1)} %get-tuple-element.94.order_ref), channel_id=1, source_target_pairs={{4,8},{8,4},{0,1},{12,13},{5,9},{9,5},{1,0},{13,12},{6,10},{10,6},... | collective-permute-start | bytes 983048 | tf_op jit(solution)/shard_map/ppermute | solution.py:539
  76.2 13.1 %collective-permute-start.24 = (bf16[640,256]{1,0:T(8,128)(2,1)S(1)}, bf16[640,256]{1,0:T(8,128)(2,1)S(1)}, u32[]{:S(2)}, u32[]{:S(2)}) collective-permute-start(bf16[640,256]{1,0:T(8,128)(2,1)S(1)} %shard_map.100.order_ref.sent_ref), channel_id=1, source_target_pairs={{0,4},{4,0},{8,12},{12,8},{1,5},{5,1},{9,13},{13,9},{2,6},{6,2},{1... | collective-permute-start | bytes 983048 | tf_op jit(solution)/shard_map/ppermute | solution.py:532
  80.1 12.7 %collective-permute-start.23 = (bf16[640,256]{1,0:T(8,128)(2,1)S(1)}, bf16[640,256]{1,0:T(8,128)(2,1)S(1)}, u32[]{:S(2)}, u32[]{:S(2)}) collective-permute-start(bf16[640,256]{1,0:T(8,128)(2,1)S(1)} %shard_map.103.order_ref.sent_ref), channel_id=1, source_target_pairs={{0,4},{4,0},{8,12},{12,8},{1,5},{5,1},{9,13},{13,9},{2,6},{6,2},{1... | collective-permute-start | bytes 983048 | tf_op jit(solution)/shard_map/ppermute | solution.py:532
  96.4 3.6 %collective-permute-start.25 = (f32[8,128]{1,0:T(8,128)S(1)}, f32[8,128]{1,0:T(8,128)S(1)}, u32[]{:S(2)}, u32[]{:S(2)}) collective-permute-start(f32[8,128]{1,0:T(8,128)S(1)} %get-tuple-element.102), channel_id=1, source_target_pairs={{0,4},{4,0},{8,12},{12,8},{1,5},{5,1},{9,13},{13,9},{2,6},{6,2},{1... | collective-permute-start | bytes 12296 | tf_op jit(solution)/shard_map/ppermute | solution.py:614
  96.5 3.5 %collective-permute-start.26 = (f32[8,128]{1,0:T(8,128)S(1)}, f32[8,128]{1,0:T(8,128)S(1)}, u32[]{:S(2)}, u32[]{:S(2)}) collective-permute-start(f32[8,128]{1,0:T(8,128)S(1)} %get-tuple-element.103), channel_id=1, source_target_pairs={{0,8},{4,12},{8,0},{12,4},{1,9},{5,13},{9,1},{13,5},{2,10},{6,14},... | collective-permute-start | bytes 12296 | tf_op jit(solution)/shard_map/ppermute | solution.py:614
  98.6 4.3 %collective-permute-start.27 = (f32[8,128]{1,0:T(8,128)S(1)}, f32[8,128]{1,0:T(8,128)S(1)}, u32[]{:S(2)}, u32[]{:S(2)}) collective-permute-start(f32[8,128]{1,0:T(8,128)S(1)} %get-tuple-element.104), channel_id=1, source_target_pairs={{0,12},{4,8},{8,4},{12,0},{1,13},{5,9},{9,5},{13,1},{2,14},{6,10},... | collective-permute-start | bytes 12296 | tf_op jit(solution)/shard_map/ppermute | solution.py:614
  102.9 4.2 %collective-permute-start.28 = (f32[8,128]{1,0:T(8,128)S(1)}, f32[8,128]{1,0:T(8,128)S(1)}, u32[]{:S(2)}, u32[]{:S(2)}) collective-permute-start(f32[8,128]{1,0:T(8,128)S(1)} %shard_map.108.refs_0_), channel_id=1, source_target_pairs={{0,1},{1,0},{2,3},{3,2},{4,5},{5,4},{6,7},{7,6},{8,9},{9,8},{10,11... | collective-permute-start | bytes 12296 | tf_op jit(solution)/shard_map/ppermute | solution.py:619
  105.4 2.5 %collective-permute-start.29 = (f32[8,128]{1,0:T(8,128)S(1)}, f32[8,128]{1,0:T(8,128)S(1)}, u32[]{:S(2)}, u32[]{:S(2)}) collective-permute-start(f32[8,128]{1,0:T(8,128)S(1)} %shard_map.108.refs_0_), channel_id=1, source_target_pairs={{0,2},{1,3},{2,0},{3,1},{4,6},{5,7},{6,4},{7,5},{8,10},{9,11},{10,... | collective-permute-start | bytes 12296 | tf_op jit(solution)/shard_map/ppermute | solution.py:619
  106.6 3.0 %collective-permute-start.30 = (f32[8,128]{1,0:T(8,128)S(1)}, f32[8,128]{1,0:T(8,128)S(1)}, u32[]{:S(2)}, u32[]{:S(2)}) collective-permute-start(f32[8,128]{1,0:T(8,128)S(1)} %shard_map.108.refs_0_), channel_id=1, source_target_pairs={{0,3},{1,2},{2,1},{3,0},{4,7},{5,6},{6,5},{7,4},{8,11},{9,10},{10,... | collective-permute-start | bytes 12296 | tf_op jit(solution)/shard_map/ppermute | solution.py:619
